TPU v7x, 512 devices: a whole 4x8x8 slice. The times are simulated.
512 devices in a mesh: ctx: 64 (over y, z), head: 8 (over x, core).
Axes of the slice: x: 4, y: 8, z: 8, core: 2. Of those that a mesh axis runs over, the one named last changes fastest.
Arguments:
- x_in: bfloat16 [16384, 4096], P('ctx', 'head'), may hold values from -6 to 6
- gate_z: bfloat16 [16384, 4096], P('ctx', 'head'), may hold values from -6 to 6
- b_in: bfloat16 [16384, 1024], P('ctx', 'head'), may hold values from -6 to 6
- c_in: bfloat16 [16384, 1024], P('ctx', 'head'), may hold values from -1.25 to 1.25
- step_size: float32 [64, 16384], P('head', 'ctx'), may hold values from 0.00390625 to 0.015625
- log_decay: float32 [64, 16384], P('head', 'ctx'), may hold values from 0 to 1.05
- d_skip: float32 [64], P('head'), may hold values from 0.5 to 1.5
- norm_gain: bfloat16 [4096], P('head'), may hold values from 0.5 to 1.5
- query: bfloat16 [16384, 4096], P('ctx', 'head'), may hold values from -8 to 8
- key: bfloat16 [16384, 1024], P('ctx', 'head'), may hold values from -8 to 8
- value: bfloat16 [16384, 1024], P('ctx', 'head'), may hold values from -6 to 6
- o_weight: bfloat16 [4096, 4096], P('head', 'ctx'), may hold values from -0.25 to 0.25
Outputs:
- ssm_out: bfloat16 [16384, 4096], P('ctx', 'head')
- attn_out: bfloat16 [16384, 4096], P('ctx', 'head')
All inputs are finite; a program needn't handle non-finite values.
Results may differ from a plain program's by a relative error of at most 0.023.
Values may be sent and summed in bfloat16 or wider, within the bound.
A program may use at most 128 MiB of HBM per device.

v0:
```python
import jax
import jax.numpy as jnp
from jax import lax
from jax.sharding import PartitionSpec as P

MIXER_HEADS = 64
MDIM = 64
NSTATE = 128
GROUPS = 8
AHEADS = 32
KVG = 8
ADH = 128


def entering(value, axis, join, neutral):
    place = lax.axis_index(axis)
    gathered = jax.tree.map(
        lambda a, kind: lax.all_gather(a.astype(kind), axis), value, (jnp.bfloat16, jnp.bfloat16)
    )
    state = jax.tree.map(lambda a, e: jnp.zeros_like(a) + jnp.asarray(e, a.dtype), value, neutral)

    def one(lap, state):
        return join(
            state,
            jax.tree.map(
                lambda a, own: lax.dynamic_index_in_dim(a, lap, 0, False).astype(own.dtype),
                gathered,
                value,
            ),
        )

    return lax.fori_loop(0, place, one, state)


def combine_states(earlier, later):
    return (earlier[0] * later[0], later[0][:, None, None] * earlier[1] + later[1])


def mixer_block(x_in, gate_z, b_in, c_in, step_size, log_decay, d_skip, norm_gain):
    tok_rows = x_in.shape[0]
    per_group = MIXER_HEADS // GROUPS
    groups_here = b_in.shape[1] // NSTATE
    heads_here = groups_here * per_group
    values = x_in.reshape(tok_rows, heads_here, MDIM)
    inputs_b = b_in.reshape(tok_rows, groups_here, NSTATE)
    inputs_c = c_in.reshape(tok_rows, groups_here, NSTATE)
    summed = jnp.cumsum(log_decay, axis=1)
    causal = (
        jnp.arange(tok_rows, dtype=jnp.int32)[:, None]
        >= jnp.arange(tok_rows, dtype=jnp.int32)[None, :]
    )
    scores = jnp.einsum("tgn,ugn->gtu", inputs_c, inputs_b, preferred_element_type=jnp.float32)
    scores = jnp.repeat(scores, per_group, axis=0)
    spread = jnp.where(causal[None], summed[:, :, None] - summed[:, None, :], 0.0)
    mixing = jnp.where(causal[None], jnp.exp(-spread) * scores * step_size[:, None, :], 0.0).astype(
        jnp.bfloat16
    )
    inner = jnp.einsum("htu,uhp->thp", mixing, values, preferred_element_type=jnp.float32)
    tail = jnp.exp(summed - summed[:, -1:]) * step_size
    scaled_b = (
        jnp.repeat(inputs_b, per_group, axis=1).astype(jnp.float32) * tail.T[:, :, None]
    ).astype(jnp.bfloat16)
    local = jnp.einsum("thn,thp->hnp", scaled_b, values, preferred_element_type=jnp.float32)
    through = jnp.exp(-summed[:, -1])
    identity = (jnp.ones_like(through), jnp.zeros_like(local))
    incoming = entering((through, local), "ctx", combine_states, identity)[1]
    wide_c = jnp.repeat(inputs_c, per_group, axis=1).astype(jnp.float32)
    carried = jnp.einsum("thn,hnp->thp", wide_c, incoming, precision=lax.Precision.HIGHEST)
    carried = carried * jnp.exp(-summed).T[:, :, None]
    result = inner + carried + d_skip[None, :, None] * values.astype(jnp.float32)
    gated = result * jax.nn.silu(gate_z.astype(jnp.float32).reshape(tok_rows, heads_here, MDIM))
    grouped = gated.reshape(tok_rows, groups_here, per_group * MDIM)
    normed = grouped * lax.rsqrt(jnp.mean(grouped * grouped, axis=-1, keepdims=True) + 1e-05)
    return (normed.reshape(tok_rows, heads_here * MDIM) * norm_gain.astype(jnp.float32)).astype(
        jnp.bfloat16
    )


def attention_block(query, key, value):
    tok_rows = query.shape[0]
    share = AHEADS // KVG
    groups_here = key.shape[1] // ADH
    scale = ADH ** (-0.5)
    first_row = lax.axis_index("ctx") * tok_rows
    queries = query.reshape(tok_rows, groups_here, share, ADH)
    own_rows = first_row + jnp.arange(tok_rows, dtype=jnp.int32)
    span = tok_rows * max(1, 512 // tok_rows)

    def update(carry, keys_part, values_part, begin):
        peak, total, gathered = carry
        width = keys_part.shape[0]
        keys_view = keys_part.reshape(width, groups_here, ADH)
        values_view = values_part.reshape(width, groups_here, ADH)
        scores = (
            jnp.einsum("tgqd,ugd->gqtu", queries, keys_view, preferred_element_type=jnp.float32)
            * scale
        )
        allowed = own_rows[:, None] >= (begin + jnp.arange(width, dtype=jnp.int32))[None, :]
        scores = jnp.where(allowed, scores, -1e30)
        new_peak = jnp.maximum(peak, jnp.max(scores, axis=-1))
        weights = jnp.where(allowed, jnp.exp(scores - new_peak[..., None]), 0.0)
        shrink = jnp.exp(peak - new_peak)
        total = total * shrink + jnp.sum(weights, axis=-1)
        product = jnp.einsum(
            "gqtu,ugd->gqtd",
            weights.astype(jnp.bfloat16),
            values_view,
            preferred_element_type=jnp.float32,
        )
        gathered = gathered * shrink[..., None] + product
        return (new_peak, total, gathered)

    initial = (
        jnp.full((groups_here, share, tok_rows), -1e30, jnp.float32),
        jnp.zeros((groups_here, share, tok_rows), jnp.float32),
        jnp.zeros((groups_here, share, tok_rows, ADH), jnp.float32),
    )
    keys_in = lax.all_gather(key, "ctx", axis=0, tiled=True)
    values_in = lax.all_gather(value, "ctx", axis=0, tiled=True)
    count = keys_in.shape[0]

    def visit(index, state):
        offset = index * span
        keys_part = lax.dynamic_slice_in_dim(keys_in, offset, span, 0)
        values_part = lax.dynamic_slice_in_dim(values_in, offset, span, 0)
        return update(state, keys_part, values_part, offset)

    peak, total, gathered = lax.fori_loop(0, count // span, visit, initial)
    heads = (gathered / total[..., None]).astype(jnp.bfloat16)
    return heads.transpose(2, 0, 1, 3).reshape(tok_rows, groups_here * share * ADH)


def per_device(
    x_in, gate_z, b_in, c_in, step_size, log_decay, d_skip, norm_gain, query, key, value, o_weight
):
    ssm_out = mixer_block(x_in, gate_z, b_in, c_in, step_size, log_decay, d_skip, norm_gain)
    heads = attention_block(query, key, value)
    terms = jnp.dot(
        heads,
        lax.all_gather(o_weight, "ctx", axis=1, tiled=True),
        preferred_element_type=jnp.float32,
    )
    attn_out = lax.psum_scatter(terms.astype(jnp.bfloat16), "head", scatter_dimension=1, tiled=True)
    return (ssm_out, attn_out)


def solution(mesh):
    in_specs = (
        P("ctx", "head"),
        P("ctx", "head"),
        P("ctx", "head"),
        P("ctx", "head"),
        P("head", "ctx"),
        P("head", "ctx"),
        P("head"),
        P("head"),
        P("ctx", "head"),
        P("ctx", "head"),
        P("ctx", "head"),
        P("head", "ctx"),
    )
    out_specs = (P("ctx", "head"), P("ctx", "head"))
    return jax.shard_map(
        per_device, mesh=mesh, in_specs=in_specs, out_specs=out_specs, check_vma=False
    )
```

profile of v0, /device:TPU:504, one launch (start us, length us, event | category | flops | bytes accessed | tf_op | source)
XLA Modules:
  0.0 546.7 jit_solution(3660937341798634546)
XLA Ops:
  16.4 77.4 %all-gather.7.cloned.1.call-done = bf16[16384,128]{1,0:T(8,128)(2,1)} async-done(((bf16[256,128]{1,0:T(8,128)(2,1)}), bf16[16384,128]{1,0:T(8,128)(2,1)}) %all-gather.7.cloned.1.call-update) | async-done | bytes 4194320 | tf_op jit(solution)/shard_map/all_gather | solution.py:118
  93.9 86.9 %all-gather.9.cloned.1.call-done = bf16[16384,128]{1,0:T(8,128)(2,1)} async-done(((bf16[256,128]{1,0:T(8,128)(2,1)}), bf16[16384,128]{1,0:T(8,128)(2,1)}) %all-gather.9.cloned.1.call-update) | async-done | bytes 4194320 | tf_op jit(solution)/shard_map/all_gather | solution.py:119
  180.7 127.3 %while.31 = (s32[]{:T(128)}, f32[1,4,256]{2,1,0:T(4,128)S(1)}, f32[1,4,256]{2,1,0:T(4,128)S(1)}, f32[1,4,256,128]{3,2,1,0:T(8,128)S(1)}, bf16[16384,128]{1,0:T(8...) while((s32[]{:T(128)}, f32[1,4,256]{2,1,0:T(4,128)S(1)}, ...), condition=%wide.region_8.9_spmd.clone, body=%wide.region_5.8_spmd.clone.sunk | while | flops 275782400 | bytes 8460479 | solution.py:128
  186.3 1.8 fusion.59
  190.3 1.8 fusion.59
  194.3 1.8 fusion.59
  198.2 1.8 fusion.59
  202.2 1.8 fusion.59
  206.2 1.8 fusion.59
  214.2 1.8 fusion.59
  222.1 1.8 fusion.59
  226.1 1.8 fusion.59
  230.1 1.8 fusion.59
  234.1 1.8 fusion.59
  238.0 1.8 fusion.59
  242.0 1.8 fusion.59
  246.0 1.8 fusion.59
  250.0 1.8 fusion.59
  254.0 1.8 fusion.59
  257.9 1.8 fusion.59
  261.9 1.8 fusion.59
  265.9 1.8 fusion.59
  269.9 1.8 fusion.59
  273.9 1.8 fusion.59
  277.9 1.8 fusion.59
  285.8 1.8 fusion.59
  289.8 1.8 fusion.59
  293.8 1.8 fusion.59
  301.7 1.8 fusion.59
  308.4 4.9 convolution_convert_fusion
  315.7 138.7 %all-reduce = bf16[512]{0:T(512)(128)(2,1)S(1)} all-reduce(bf16[512]{0:T(512)(128)(2,1)S(1)} %dynamic-update-slice), channel_id=2, replica_groups=mesh['ctx'=64,'head'=8] {'ctx'}, use_global_device_ids=true, to_apply=%add | all-reduce | flops 512 | bytes 2048
  455.0 82.6 %while.30 = (s32[]{:T(128)}, f32[8,128,64]{2,1,0:T(8,128)S(1)}, s32[]{:T(128)}, bf16[64,8]{1,0:T(8,128)(2,1)S(1)}, bf16[64,8,128,64]{2,3,1,0:T(8,128)(2,1)}, /*index=5*/s32[]{:T(128)}, s32[]{:T(128)}, s32[]{:T(128)}) while((s32[]{:T(128)}, f32[8,128,64]{2,1,0:T(8,128)S(1)}, s32[]{:T(128)}, bf16[64,8]{1,0:T(8,128)(2,1)S(1)}, ...), condition=%wide.region_3.4_spmd, body=%wide.region_2.3_spmd.sunk | while | flops 196621 | bytes 1179855 | solution.py:32
  (571 shorter events, 172.3 us)
Async XLA Ops:
  7.2 447.5 %copy-start = (bf16[256,128]{1,0:T(8,128)(2,1)S(1)}, bf16[256,128]{1,0:T(8,128)(2,1)}, u32[]{:S(2)}) copy-start(bf16[256,128]{1,0:T(8,128)(2,1)} %param.19) | copy-start | bytes 196612
  7.2 86.7 %all-gather.7.cloned.1.call-start = ((), (), s32[]{:S(2)}) async-start(), calls=%async_computation.1 | async-start | bytes 4259840 | tf_op jit(solution)/shard_map/all_gather | solution.py:118
  7.9 172.8 %all-gather.9.cloned.1.call-start = ((), (), s32[]{:S(2)}) async-start(), calls=%async_computation.2 | async-start | bytes 4259840 | tf_op jit(solution)/shard_map/all_gather | solution.py:119
  8.7 299.7 %all-gather.11.cloned.1.call-start = ((), (), s32[]{:S(2)}) async-start(), calls=%async_computation.3 | async-start | bytes 4259840 | tf_op jit(solution)/shard_map/all_gather | solution.py:140
  9.4 445.5 %all-gather.13.cloned.1.call-start = ((), (), s32[]{:S(2)}) async-start(), calls=%async_computation.5 | async-start | bytes 8519680 | tf_op jit(solution)/shard_map/all_gather | solution.py:18
  15.1 525.1 %reduce-scatter.2.cloned.1.call-start = ((), (), s32[]{:S(2)}) async-start(), calls=%async_computation.4 | async-start | bytes 2359296 | tf_op jit(solution)/shard_map/reduce_scatter | solution.py:143
  313.3 141.2 %copy-start.1 = (bf16[256,512]{1,0:T(8,128)(2,1)S(1)}, bf16[256,512]{1,0:T(8,128)(2,1)}, u32[]{:S(2)}) copy-start(bf16[256,512]{1,0:T(8,128)(2,1)} %param.17) | copy-start | bytes 786436
  313.3 141.4 %copy-start.4 = (bf16[512]{0:T(512)(128)(2,1)S(1)}, bf16[512]{0:T(512)(128)(2,1)}, u32[]{:S(2)}) copy-start(bf16[512]{0:T(512)(128)(2,1)} %param.23) | copy-start | bytes 3076
  313.3 141.4 %copy-start.2 = (bf16[256,128]{1,0:T(8,128)(2,1)S(1)}, bf16[256,128]{1,0:T(8,128)(2,1)}, u32[]{:S(2)}) copy-start(bf16[256,128]{1,0:T(8,128)(2,1)} %param.18) | copy-start | bytes 196612
  455.0 83.3 %copy-start.3 = (f32[8,256]{1,0:T(8,128)S(1)}, f32[8,256]{1,0:T(8,128)}, u32[]{:S(2)}) copy-start(f32[8,256]{1,0:T(8,128)} %param.20) | copy-start | bytes 24580
  455.0 83.3 %copy-start.5 = (f32[8]{0:T(128)S(1)}, f32[8]{0:T(128)}, u32[]{:S(2)}) copy-start(f32[8]{0:T(128)} %param.22) | copy-start | bytes 100
Sparse Core Ops, SparseCore 0:
  11.0 82.7 all-gather.6
  96.9 83.8 all-gather.8
  183.8 83.8 all-gather.10
  271.1 97.9 all-gather.12
  372.3 39.7 reduce-scatter.1
where the time goes:
time: 549 us; the launch traced here: 547 us
  waiting for transfers between devices  166 us (30%)
  blocking collectives  139 us (25%)
  matrix products  110 us (20%)
  local copies, waits for them, and re-layouts  74.2 us (14%)
  other arithmetic  37.4 us (7%)
  between operations  14.7 us (3%)
    unnamed x1, blocking collectives  139 us
    all_gather x1, waiting for transfers between devices, attention_block(): values_in = lax.all_gather(value, 'ctx', axis=0, tiled=True)  86.9 us
    all_gather x1, waiting for transfers between devices, attention_block(): keys_in = lax.all_gather(key, 'ctx', axis=0, tiled=True)  77.4 us
    dynamic_slice x126, local copies, waits for them, and re-layouts, one(): lax.dynamic_index_in_dim(a, lap, 0, False).astype(own.dtype)  69.2 us
    dot_general x32, matrix products, update(): jnp.einsum('gqtu,ugd->gqtd', weights.astype(jnp.bfloat16), values_view, p...  57.6 us
    dot_general x32, matrix products, update(): jnp.einsum('tgqd,ugd->gqtu', queries, keys_view, preferred_element_type=j...  44.7 us
    reduce_sum x32, other arithmetic, update(): total = total * shrink + jnp.sum(weights, axis=-1)  17 us
  transfers between devices with their start and end apart: 5, of which 2 were waited for; matrix products, arithmetic and copies ran while one was open for 41% of the time, Pallas kernels for 0%

commit v1 on v0

v1 whole, which is shorter than its diff:
```python
import functools
import math

import jax
import jax.numpy as jnp
from jax import lax
from jax.experimental import pallas as pl
from jax.experimental.pallas import tpu as pltpu
from jax.sharding import PartitionSpec as P

MESH = pl.DeviceIdType.MESH
BF = jnp.bfloat16
F32 = jnp.float32
TOK = 256
HALF = TOK // 2
ADH = 128
SHARE = 4
RING = 8
XS = 4
NEG = -1e30
SCALE = math.log2(math.e) / math.sqrt(ADH)
NT = (((1,), (1,)), ((), ()))


def mod(a, n):
    return lax.rem(a + 2 * n, n)


def dot(a, b):
    return jnp.dot(a, b, preferred_element_type=F32)


def dot_nt(a, b, precision=None):
    return lax.dot_general(a, b, NT, precision=precision, preferred_element_type=F32)


def kernel(
    x_ref, gate_ref, b_ref, c_ref, step_ref, decay_ref, skip_ref, gain_ref, q_ref, k_ref, v_ref, wt_ref,
    ssm_ref, out_ref,
    kv, w, q4, acc, peak, heads,
    arow, scores, gated, st_out, st_in, pre, predec, tot_out, tot_in, ret_out, ret_in,
    sib_out, sib_in, mine, x1_out, x1_in, x2_out, x2_in,
    kv1_s, kv1_r, kv2_s, kv2_r, w1_s, w1_r, w2_s, w2_r,
    st_s, st_r, tot_s, tot_r, ret_s, ret_r, sib_s, sib_r, x1_s, x1_r, x2_s, x2_r,
):
    me = lax.axis_index("ctx")
    head = lax.axis_index("head")
    y, z = me // RING, me % RING
    xc, core = head // 2, head % 2
    major0, minor0 = (y, z), (z, y)

    def ctx_of(hf, major, minor):
        return major * RING + minor if hf == 0 else minor * RING + major

    barrier = pltpu.get_barrier_semaphore()

    def greet(i, _):
        pl.semaphore_signal(barrier, inc=1, device_id=(y * RING + mod(z + i, RING), head), device_id_type=MESH)
        pl.semaphore_signal(barrier, inc=1, device_id=(mod(y + i, RING) * RING + z, head), device_id_type=MESH)
        pl.semaphore_signal(barrier, inc=1, device_id=(me, mod(head + i, 8)), device_id_type=MESH)
        return 0

    lax.fori_loop(1, 8, greet, 0)

    kv[0, y, z, 0] = k_ref[:HALF]
    kv[0, y, z, 1] = v_ref[:HALF]
    kv[1, z, y, 0] = k_ref[HALF:]
    kv[1, z, y, 1] = v_ref[HALF:]
    w[0, y, z] = wt_ref[:, :256]
    w[1, z, y] = wt_ref[:, 256:]
    for a in range(SHARE):
        q4[a] = q_ref[:, a * ADH : (a + 1) * ADH]

    pl.semaphore_wait(barrier, 21)

    def first(buf, ss, rs, hf, dr, dist, arriving):
        slot = dist - 1 + (0 if dr > 0 else 4)
        block = mod(minor0[hf] - dr * (dist if arriving else dist - 1), RING)
        ref = buf.at[hf, major0[hf], block]
        to = ctx_of(hf, major0[hf], mod(minor0[hf] + dr, RING))
        return pltpu.make_async_remote_copy(
            src_ref=ref, dst_ref=ref, send_sem=ss.at[hf, slot], recv_sem=rs.at[hf, slot],
            device_id=(to, head), device_id_type=MESH,
        )

    def second(buf, ss, rs, hf, dr, item, arriving):
        dist = item // 2 + 1
        sub = jnp.where(item == 6, 0 if dr > 0 else 1, item % 2)
        major = mod(major0[hf] - dr * (dist if arriving else dist - 1), RING)
        ref = buf.at[hf, major, pl.ds(sub * 4, 4)]
        to = ctx_of(hf, mod(major0[hf] + dr, RING), minor0[hf])
        way = 0 if dr > 0 else 1
        return pltpu.make_async_remote_copy(
            src_ref=ref, dst_ref=ref, send_sem=ss.at[hf, way, item], recv_sem=rs.at[hf, way, item],
            device_id=(to, head), device_id_type=MESH,
        )

    STREAMS = [(hf, dr) for hf in (0, 1) for dr in (1, -1)]
    reach = {(0, 1): 4, (0, -1): 3, (1, 1): 3, (1, -1): 4}

    kv1 = functools.partial(first, kv, kv1_s, kv1_r)
    kv2 = functools.partial(second, kv, kv2_s, kv2_r)
    w1 = functools.partial(first, w, w1_s, w1_r)
    w2 = functools.partial(second, w, w2_s, w2_r)

    for hf, dr in STREAMS:
        kv1(hf, dr, 1, False).start()

    def weigh(a, s, v, fresh):
        n = s.shape[1]
        top = jnp.broadcast_to(jnp.max(s, axis=1, keepdims=True) * SCALE, (TOK, ADH))
        new = top if fresh else jnp.maximum(peak[a], top)
        p = jnp.exp2(s * SCALE - jnp.concatenate([new] * (n // ADH), axis=1)).astype(BF)
        pv = dot(p, jnp.concatenate([v, jnp.ones((n, ADH), BF)], axis=1))
        if fresh:
            acc[a] = pv
        else:
            shrink = jnp.exp2(peak[a] - new)
            acc[a] = acc[a] * jnp.concatenate([shrink, shrink], axis=1) + pv
        peak[a] = new

    rows = lax.broadcasted_iota(jnp.int32, (TOK, TOK), 0)
    cols = lax.broadcasted_iota(jnp.int32, (TOK, TOK), 1)
    causal = rows >= cols
    for a in range(SHARE):
        weigh(a, jnp.where(causal, dot_nt(q4[a], k_ref[...]), NEG), v_ref[...], True)

    for dist in range(1, 5):
        for hf, dr in STREAMS:
            if dist <= reach[hf, dr]:
                kv1(hf, dr, dist, True).wait_recv()
                if dist < reach[hf, dr]:
                    kv1(hf, dr, dist + 1, False).start()
    for item in (0, 1):
        for hf, dr in STREAMS:
            kv2(hf, dr, item, False).start()

    lane = lax.broadcasted_iota(jnp.int32, (1, ADH), 1) < 64

    def tri():
        return jnp.where(causal, 1.0, 0.0).astype(F32)

    def spread(pair):
        rows2 = [jnp.broadcast_to(decay_ref[pl.ds(2 * pair + i, 1), :], (64, TOK)) for i in (0, 1)]
        return dot_nt(tri(), jnp.concatenate(rows2, axis=0), lax.Precision.HIGHEST)

    def pair_columns(pair):
        return pl.ds(pl.multiple_of(pair * ADH, ADH), ADH)

    def split(vec):
        hi = vec.astype(BF)
        lo = (vec - hi.astype(F32)).astype(BF)
        return jnp.concatenate([jnp.broadcast_to(hi, (8, ADH)), jnp.broadcast_to(lo, (8, ADH))], axis=0)

    def joined(block):
        return block[64:65].astype(F32) + block[72:73].astype(F32)

    def row_copy(out, into, ss, rs, dz, arriving):
        there = mod(z + dz, RING)
        src = mod(z - dz, RING) if arriving else z
        return pltpu.make_async_remote_copy(
            src_ref=out.at[there], dst_ref=into.at[src], send_sem=ss.at[dz], recv_sem=rs.at[dz],
            device_id=(y * RING + there, head), device_id_type=MESH,
        )

    def column_copy(dy, arriving):
        there = mod(y + dy, RING)
        src = mod(y - dy, RING) if arriving else y
        return pltpu.make_async_remote_copy(
            src_ref=tot_out, dst_ref=tot_in.at[src], send_sem=tot_s.at[dy], recv_sem=tot_r.at[dy],
            device_id=(there * RING + z, head), device_id_type=MESH,
        )

    def every(f):
        def one(i, _):
            f(i)
            return 0

        lax.fori_loop(1, RING, one, 0)

    def states_out():
        arow[...] = dot_nt(decay_ref[...], tri(), lax.Precision.HIGHEST)
        bt = b_ref[...].astype(F32).T

        def one(pair, _):
            xp = x_ref[:, pair_columns(pair)]
            parts = []
            for i in (0, 1):
                a = arow[pl.ds(2 * pair + i, 1), :]
                tail = jnp.exp(a - a[:, TOK - 1 :]) * step_ref[pl.ds(2 * pair + i, 1), :]
                parts.append(dot((bt * tail).astype(BF), xp))
            state = jnp.where(lane, parts[0], parts[1]).astype(BF)
            last = [arow[pl.ds(2 * pair + i, 1), :][:, TOK - 1 :] for i in (0, 1)]
            through = split(jnp.exp(-jnp.where(lane, last[0], last[1])))
            for i in (0, 1):
                st_out[2 * pair + i, :64] = state[64 * i : 64 * i + 64]
                st_out[2 * pair + i, 64:] = through
            return 0

        lax.fori_loop(0, 4, one, 0)
        every(lambda dz: row_copy(st_out, st_in, st_s, st_r, dz, False).start())
        st_in[z] = st_out[z]

    def totals_out():
        every(lambda dz: row_copy(st_out, st_in, st_s, st_r, dz, True).wait_recv())

        def one(i, carry):
            state, decay = carry
            pre[i] = state
            predec[i] = jnp.broadcast_to(decay, (8, ADH))
            block = st_in[i]
            t = joined(block)
            return t * state + block[:64].astype(F32), t * decay

        state, decay = lax.fori_loop(0, RING, one, (jnp.zeros((64, ADH), F32), jnp.ones((1, ADH), F32)))
        tot_out[:64] = state.astype(BF)
        tot_out[64:] = split(decay)
        every(lambda dy: column_copy(dy, False).start())

    def incoming_out():
        every(lambda dy: column_copy(dy, True).wait_recv())

        def one(i, state):
            block = tot_in[i]
            return joined(block) * state + block[:64].astype(F32)

        state = lax.fori_loop(0, y, one, jnp.zeros((64, ADH), F32))

        def give(i, _):
            ret_out[i] = (pre[i] + predec[i][:1] * state).astype(BF)
            return 0

        lax.fori_loop(0, RING, give, 0)
        every(lambda dz: row_copy(ret_out, ret_in, ret_s, ret_r, dz, False).start())
        ret_in[z] = ret_out[z]

    def mix():
        every(lambda dz: row_copy(ret_out, ret_in, ret_s, ret_r, dz, True).wait_recv())
        scores[...] = dot_nt(c_ref[...], b_ref[...])

        def one(pair, squares):
            at = pair_columns(pair)
            xp = x_ref[:, at]
            a_t = spread(pair)
            parts = []
            for i in (0, 1):
                a_u = arow[pl.ds(2 * pair + i, 1), :]
                gap = jnp.where(causal, a_u - a_t[:, 64 * i : 64 * i + 1], NEG)
                mixing = jnp.exp(gap) * (scores[...] * step_ref[pl.ds(2 * pair + i, 1), :])
                parts.append(dot(mixing.astype(BF), xp))
            carried = dot(c_ref[...], ret_in[pl.ds(2 * pair, 2)].reshape(ADH, ADH)) * jnp.exp(-a_t)
            skip = jnp.where(lane, skip_ref[2 * pair], skip_ref[2 * pair + 1])
            total = jnp.where(lane, parts[0], parts[1]) + carried + skip * xp.astype(F32)
            g = gate_ref[:, at].astype(F32)
            total = total * (g / (1.0 + jnp.exp(-g)))
            gated[:, at] = total
            return squares + jnp.sum(total * total, axis=1, keepdims=True)

        squares = lax.fori_loop(0, 4, one, jnp.zeros((TOK, 1), F32))
        norm = lax.rsqrt(squares / 512.0 + 1e-05)
        ssm_ref[...] = (gated[...] * norm * gain_ref[...].astype(F32)).astype(BF)

    def attend(step):
        def one(st, _):
            hf = st // 2
            late = st % 2
            dist = (step + 1) // 2
            dr = 1 - 2 * late
            base = jnp.where(hf == 0, y, z)
            major = mod(base - dr * dist, RING)
            sub = jnp.where((step == 0) | (step == 7), late, (step + 1) % 2)
            stride = jnp.where(hf == 0, 1, RING)
            u0 = jnp.where(hf == 0, major * RING + sub * 4, sub * 4 * RING + major)

            @pl.when(u0 < me)
            def _():
                keys = kv[hf, major, pl.ds(sub * 4, 4), 0].reshape(4 * HALF, ADH)
                values = kv[hf, major, pl.ds(sub * 4, 4), 1].reshape(4 * HALF, ADH)
                block = lax.broadcasted_iota(jnp.int32, (1, 4 * HALF), 1) // HALF
                bias = jnp.where(u0 + block * stride < me, 0.0, NEG)
                for a in range(SHARE):
                    weigh(a, dot_nt(q4[a], keys) + bias, values, False)

            return 0

        lax.fori_loop(0, 4, one, 0)

    def pass_on(copy, item):
        for hf, dr in STREAMS:
            copy(hf, dr, item, True).wait_recv()

            @pl.when(item < (5 if dr > 0 else 4))
            def _(hf=hf, dr=dr):
                copy(hf, dr, jnp.minimum(item + 2, 6), False).start()

            if dr < 0:

                @pl.when(item == 5)
                def _(hf=hf, dr=dr):
                    copy(hf, dr, 6, False).start()

    def step(i, _):
        @pl.when(i >= 1)
        def _():
            pass_on(kv2, i - 1)

        for hf, dr in STREAMS:
            far = reach[hf, dr]

            @pl.when((i >= 1) & (i <= far))
            def _(hf=hf, dr=dr):
                w1(hf, dr, jnp.maximum(i, 1), True).wait_recv()

            @pl.when(i < far)
            def _(hf=hf, dr=dr):
                w1(hf, dr, i + 1, False).start()

        @pl.when(i == 6)
        def _():
            for item in (0, 1):
                for hf, dr in STREAMS:
                    w2(hf, dr, item, False).start()

        pl.when(i == 0)(states_out)
        pl.when(i == 1)(totals_out)
        pl.when(i == 2)(incoming_out)
        pl.when(i == 3)(mix)
        attend(i)
        return 0

    lax.fori_loop(0, 8, step, 0)

    for a in range(SHARE):
        heads[:, a * ADH : (a + 1) * ADH] = (acc[a][:, :ADH] / acc[a][:, ADH:]).astype(BF)

    def w_step(i, _):
        pass_on(w2, i)
        return 0

    lax.fori_loop(0, 7, w_step, 0)

    def product(f):
        left = dot_nt(heads[:, :256], w[0, f].reshape(512, 256))
        right = dot_nt(heads[:, 256:], w[1, :, f].reshape(512, 256))
        return (left + right).astype(BF)

    def sib_copy(o):
        return pltpu.make_async_remote_copy(
            src_ref=sib_out.at[o], dst_ref=sib_in.at[o], send_sem=sib_s.at[o], recv_sem=sib_r.at[o],
            device_id=(me, 2 * xc + 1 - core), device_id_type=MESH,
        )

    def side(way):
        return (me, 2 * mod(xc + (1 if way == 0 else -1), XS) + core)

    def x1_copy(way):
        return pltpu.make_async_remote_copy(
            src_ref=x1_out.at[way], dst_ref=x1_in.at[way], send_sem=x1_s.at[way], recv_sem=x1_r.at[way],
            device_id=side(way), device_id_type=MESH,
        )

    def x2_copy(way):
        return pltpu.make_async_remote_copy(
            src_ref=x2_out.at[way], dst_ref=x2_in.at[way], send_sem=x2_s.at[way], recv_sem=x2_r.at[way],
            device_id=side(way), device_id_type=MESH,
        )

    for o in (2, 1, 3, 0):
        chip = mod(xc + o, XS)
        sib_out[o] = product(2 * chip + 1 - core)
        sib_copy(o).start()
        mine[o] = product(2 * chip + core)

    def both(o, lo, hi):
        return mine[o, lo:hi].astype(F32) + sib_in[o, lo:hi].astype(F32)

    sib_copy(2).wait_recv()
    x1_out[0] = both(2, 0, HALF).astype(BF)
    x1_copy(0).start()
    x1_out[1] = both(2, HALF, TOK).astype(BF)
    x1_copy(1).start()
    sib_copy(1).wait_recv()
    x2_out[0, HALF:] = both(1, HALF, TOK).astype(BF)
    x1_copy(0).wait_recv()
    x2_out[0, :HALF] = (both(1, 0, HALF) + x1_in[0].astype(F32)).astype(BF)
    x2_copy(0).start()
    sib_copy(3).wait_recv()
    x2_out[1, :HALF] = both(3, 0, HALF).astype(BF)
    x1_copy(1).wait_recv()
    x2_out[1, HALF:] = (both(3, HALF, TOK) + x1_in[1].astype(F32)).astype(BF)
    x2_copy(1).start()
    sib_copy(0).wait_recv()
    x2_copy(0).wait_recv()
    x2_copy(1).wait_recv()
    out_ref[...] = (both(0, 0, TOK) + x2_in[0].astype(F32) + x2_in[1].astype(F32)).astype(BF)

    for hf, dr in STREAMS:
        for dist in range(1, reach[hf, dr] + 1):
            kv1(hf, dr, dist, False).wait_send()
            w1(hf, dr, dist, False).wait_send()

        def sent(item, _, hf=hf, dr=dr):
            kv2(hf, dr, item, False).wait_send()
            w2(hf, dr, item, False).wait_send()
            return 0

        lax.fori_loop(0, 7, sent, 0)
    every(lambda d: row_copy(st_out, st_in, st_s, st_r, d, False).wait_send())
    every(lambda d: column_copy(d, False).wait_send())
    every(lambda d: row_copy(ret_out, ret_in, ret_s, ret_r, d, False).wait_send())
    for o in range(4):
        sib_copy(o).wait_send()
    for way in (0, 1):
        x1_copy(way).wait_send()
        x2_copy(way).wait_send()


def per_device(
    x_in, gate_z, b_in, c_in, step_size, log_decay, d_skip, norm_gain, query, key, value, o_weight
):
    vmem = pl.BlockSpec(memory_space=pltpu.VMEM)
    smem = pl.BlockSpec(memory_space=pltpu.SMEM)
    dma = pltpu.SemaphoreType.DMA
    tokens = (TOK, 512)
    return pl.pallas_call(
        kernel,
        out_shape=(jax.ShapeDtypeStruct(tokens, BF), jax.ShapeDtypeStruct(tokens, BF)),
        in_specs=[vmem] * 6 + [smem] + [vmem] * 5,
        out_specs=(vmem, vmem),
        scratch_shapes=[
            pltpu.VMEM((2, RING, RING, 2, HALF, ADH), BF),
            pltpu.VMEM((2, RING, RING, 64, 256), BF),
            pltpu.VMEM((SHARE, TOK, ADH), BF),
            pltpu.VMEM((SHARE, TOK, 2 * ADH), F32),
            pltpu.VMEM((SHARE, TOK, ADH), F32),
            pltpu.VMEM(tokens, BF),
            pltpu.VMEM((8, TOK), F32),
            pltpu.VMEM((TOK, TOK), F32),
            pltpu.VMEM(tokens, F32),
            pltpu.VMEM((RING, 80, ADH), BF),
            pltpu.VMEM((RING, 80, ADH), BF),
            pltpu.VMEM((RING, 64, ADH), F32),
            pltpu.VMEM((RING, 8, ADH), F32),
            pltpu.VMEM((80, ADH), BF),
            pltpu.VMEM((RING, 80, ADH), BF),
            pltpu.VMEM((RING, 64, ADH), BF),
            pltpu.VMEM((RING, 64, ADH), BF),
            pltpu.VMEM((XS,) + tokens, BF),
            pltpu.VMEM((XS,) + tokens, BF),
            pltpu.VMEM((XS,) + tokens, BF),
            pltpu.VMEM((2, HALF, 512), BF),
            pltpu.VMEM((2, HALF, 512), BF),
            pltpu.VMEM((2,) + tokens, BF),
            pltpu.VMEM((2,) + tokens, BF),
            dma((2, 8)), dma((2, 8)), dma((2, 2, 7)), dma((2, 2, 7)),
            dma((2, 8)), dma((2, 8)), dma((2, 2, 7)), dma((2, 2, 7)),
            dma((8,)), dma((8,)), dma((8,)), dma((8,)), dma((8,)), dma((8,)),
            dma((4,)), dma((4,)), dma((2,)), dma((2,)), dma((2,)), dma((2,)),
        ],
        compiler_params=pltpu.CompilerParams(
            collective_id=0, has_side_effects=True, vmem_limit_bytes=48 * 1024 * 1024
        ),
        name="mixer_and_attention",
    )(
        x_in, gate_z, b_in, c_in, step_size, log_decay, d_skip, norm_gain.reshape(1, 512),
        query, key, value, o_weight.T,
    )


def solution(mesh):
    in_specs = (
        P("ctx", "head"),
        P("ctx", "head"),
        P("ctx", "head"),
        P("ctx", "head"),
        P("head", "ctx"),
        P("head", "ctx"),
        P("head"),
        P("head"),
        P("ctx", "head"),
        P("ctx", "head"),
        P("ctx", "head"),
        P("head", "ctx"),
    )
    out_specs = (P("ctx", "head"), P("ctx", "head"))
    return jax.shard_map(
        per_device, mesh=mesh, in_specs=in_specs, out_specs=out_specs, check_vma=False
    )
```

time: 549 us -> 135 us (0.25)
  the two profiles are of different devices: /device:TPU:504 before, /device:TPU:1 now
where the time goes in v1:
time: 135 us; the launch traced here: 134 us
  Pallas kernels  122 us (90%)
  local copies, waits for them, and re-layouts  11.2 us (8%)
    pallas_call x1, Pallas kernels, per_device(): pl.pallas_call(kernel, out_shape=(jax.ShapeDtypeStruct(tokens, BF), jax.S...  122 us
    unnamed x26, local copies, waits for them, and re-layouts  11.2 us

profile of v1, /device:TPU:1, one launch (start us, length us, event | category | flops | bytes accessed | tf_op | source)
XLA Modules:
  0.0 134.1 jit_solution(5602498099310240123)
XLA Ops:
  0.6 0.0 copy-start.11
  0.6 0.7 copy-done.11
  1.3 0.0 copy-start.10
  1.3 0.6 copy-done.10
  2.0 0.0 copy-start
  2.0 0.9 copy-done
  2.9 0.0 copy-start.1
  2.9 0.9 copy-done.1
  3.9 0.0 copy-start.2
  3.9 0.9 copy-done.2
  4.8 0.0 copy-start.3
  4.8 0.8 copy-done.3
  5.7 0.0 copy-start.4
  5.7 0.8 copy-done.4
  6.5 0.0 copy-start.5
  6.5 0.8 copy-done.5
  7.3 0.0 copy-start.6
  7.3 0.8 copy-done.6
  8.2 0.0 copy-start.7
  8.2 0.8 copy-done.7
  9.0 0.0 copy-start.8
  9.0 0.7 copy-done.8
  9.7 0.0 copy-start.9
  9.7 0.7 copy-done.9
  10.4 122.3 %mixer_and_attention.1 = (bf16[256,512]{1,0:T(8,128)(2,1)S(1)}, bf16[256,512]{1,0:T(8,128)(2,1)S(1)}) custom-call(bf16[256,512]{1,0:T(8,128)(2,1)S(1)} %copy-done, bf16[256,512]{1,0:T(8,128)(2,1)S(1)} %copy-done.1, bf16[256,128]{1,0:T(8,128)(2,1)S(1)} %copy-done.3, bf16[256,128]{1,0:T(8,128)(2,1)S(1)} %copy-done.4, f32[8,256]{1,0:T(8,128)S(1)} %copy-done.8, ...), custom_call_target="tpu_custom_call" | custom-call | tf_op jit(solution)/shard_map/mixer_and_attention/pallas_call | solution.py:425
  132.7 0.7 copy.16
  133.4 0.7 copy.17
  (1 shorter events, 0.0 us)
Async XLA Ops:
  0.6 0.7 copy-start.11
  1.3 0.7 copy-start.10
  2.0 0.9 copy-start
  2.9 0.9 copy-start.1
  3.9 0.9 copy-start.2
  4.8 0.8 copy-start.3
  5.7 0.8 copy-start.4
  6.5 0.8 copy-start.5
  7.3 0.8 copy-start.6
  8.2 0.8 copy-start.7
  9.0 0.7 copy-start.8
  9.7 0.7 copy-start.9

commit v2 on v1

v2 whole, which is shorter than its diff:
```python
import functools
import math

import jax
import jax.numpy as jnp
from jax import lax
from jax.experimental import pallas as pl
from jax.experimental.pallas import tpu as pltpu
from jax.sharding import PartitionSpec as P

MESH = pl.DeviceIdType.MESH
BF = jnp.bfloat16
F32 = jnp.float32
TOK = 256
HALF = TOK // 2
ADH = 128
SHARE = 4
RING = 8
XS = 4
NEG = -1e30
SCALE = math.log2(math.e) / math.sqrt(ADH)
NT = (((1,), (1,)), ((), ()))


def mod(a, n):
    return lax.rem(a + 2 * n, n)


def dot(a, b):
    return jnp.dot(a, b, preferred_element_type=F32)


def dot_nt(a, b, precision=None):
    return lax.dot_general(a, b, NT, precision=precision, preferred_element_type=F32)


def kernel(
    x_hbm, gate_hbm, b_hbm, c_hbm, step_hbm, decay_hbm, skip_ref, gain_ref, q_hbm, k_hbm, v_hbm, wt_hbm,
    ssm_ref, out_ref,
    x_ref, gate_ref, b_ref, c_ref, step_ref, decay_ref,
    kv, qs, w, acc, peak, part_o, part_l, tx_o, tx_l, rx_o, rx_l, heads,
    arow, scores, gated, squares, st_out, st_in, pre, predec, tot_out, tot_in, ret_out, ret_in,
    sib_out, sib_in, mine, x1_out, x1_in, x2_out, x2_in,
    in_s, skv_s, skv_r, sq_s, sq_r, sw_s, sw_r, kr_s, kr_r, qr_s, qr_r, o_s, o_r, l_s, l_r,
    w1_s, w1_r, w2_s, w2_r,
    st_s, st_r, tot_s, tot_r, ret_s, ret_r, sib_s, sib_r, x1_s, x1_r, x2_s, x2_r,
):
    me = lax.axis_index("ctx")
    head = lax.axis_index("head")
    y, z = me // RING, me % RING
    xc, core = head // 2, head % 2
    sibling = (me, 2 * xc + 1 - core)
    major0, minor0 = (y, z), (z, y)

    def q_place(m):
        return jnp.where(m == 0, z, y)

    def k_place(m):
        return jnp.where(m == 0, y, z)

    def ctx_at(m, q, k):
        return jnp.where(m == 0, k * RING + q, q * RING + k)

    def ctx_of(hf, major, minor):
        return major * RING + minor if hf == 0 else minor * RING + major

    barrier = pltpu.get_barrier_semaphore()

    def greet(i, _):
        pl.semaphore_signal(barrier, inc=1, device_id=(y * RING + mod(z + i, RING), head), device_id_type=MESH)
        pl.semaphore_signal(barrier, inc=1, device_id=(mod(y + i, RING) * RING + z, head), device_id_type=MESH)
        pl.semaphore_signal(barrier, inc=1, device_id=(me, mod(head + i, 8)), device_id_type=MESH)
        return 0

    lax.fori_loop(1, 8, greet, 0)

    my_k, my_q = k_place(core), q_place(core)

    def lanes(block, width):
        return pl.ds(pl.multiple_of(block * width, width), width)

    fetches = [
        (k_hbm, kv.at[core, my_k, 0]),
        (v_hbm, kv.at[core, my_k, 1]),
        (q_hbm.at[:, lanes(2 * core, ADH)], qs.at[core, my_q, 0]),
        (q_hbm.at[:, lanes(2 * core + 1, ADH)], qs.at[core, my_q, 1]),
        (wt_hbm.at[:, lanes(core, 256)], w.at[core, my_k, my_q]),
        (decay_hbm, decay_ref),
        (b_hbm, b_ref),
        (x_hbm, x_ref),
        (step_hbm, step_ref),
        (c_hbm, c_ref),
        (gate_hbm, gate_ref),
    ]
    fetches = [pltpu.make_async_copy(src, dst, in_s.at[i]) for i, (src, dst) in enumerate(fetches)]
    for fetch in fetches:
        fetch.start()
    for fetch in fetches[:2]:
        fetch.wait()
    pl.semaphore_wait(barrier, 21)

    def sib_kv(m, place):
        ref = kv.at[m, place]
        return pltpu.make_async_remote_copy(
            src_ref=ref, dst_ref=ref, send_sem=skv_s.at[place], recv_sem=skv_r.at[place],
            device_id=sibling, device_id_type=MESH,
        )

    def sib_q(m, i):
        return pltpu.make_async_remote_copy(
            src_ref=q_hbm.at[:, lanes(2 * (1 - core) + i, ADH)], dst_ref=qs.at[m, q_place(m), i],
            send_sem=sq_s.at[i], recv_sem=sq_r.at[i], device_id=sibling, device_id_type=MESH,
        )

    def sib_w(m):
        return pltpu.make_async_remote_copy(
            src_ref=wt_hbm.at[:, lanes(1 - core, 256)], dst_ref=w.at[m, k_place(m), q_place(m)],
            send_sem=sw_s, recv_sem=sw_r, device_id=sibling, device_id_type=MESH,
        )

    def ring_kv(dr, dist, arriving):
        way = 0 if dr > 0 else 1
        place = mod(my_k - dr * (dist if arriving else dist - 1), RING)
        ref = kv.at[core, place] if dist < 4 else kv.at[core, place, way]
        to = ctx_at(core, my_q, mod(my_k + dr, RING))
        return pltpu.make_async_remote_copy(
            src_ref=ref, dst_ref=ref, send_sem=kr_s.at[way, dist - 1], recv_sem=kr_r.at[way, dist - 1],
            device_id=(to, head), device_id_type=MESH,
        )

    def ring_q(m, dr, dist, arriving):
        way = 0 if dr > 0 else 1
        place = mod(q_place(m) - dr * (dist if arriving else dist - 1), RING)
        ref = qs.at[m, place] if dist < 4 else qs.at[m, place, way]
        to = ctx_at(m, mod(q_place(m) + dr, RING), k_place(m))
        return pltpu.make_async_remote_copy(
            src_ref=ref, dst_ref=ref, send_sem=qr_s.at[m, way, dist - 1], recv_sem=qr_r.at[m, way, dist - 1],
            device_id=(to, head), device_id_type=MESH,
        )

    def kv_hop(dist):
        for dr in (1, -1):
            ring_kv(dr, dist, True).wait_recv()
            if dist < 4:
                ring_kv(dr, dist + 1, False).start()
                sib_kv(core, mod(my_k - dr * dist, RING)).start()
        if dist == 4:
            sib_kv(core, mod(my_k + 4, RING)).start()

    def q_hop(dist):
        for m in (0, 1):
            for dr in (1, -1):
                if dist > 0:
                    ring_q(m, dr, dist, True).wait_recv()
                if dist < 4:
                    ring_q(m, dr, dist + 1, False).start()

    def first(buf, ss, rs, hf, dr, dist, arriving):
        slot = dist - 1 + (0 if dr > 0 else 4)
        block = mod(minor0[hf] - dr * (dist if arriving else dist - 1), RING)
        ref = buf.at[hf, major0[hf], block]
        to = ctx_of(hf, major0[hf], mod(minor0[hf] + dr, RING))
        return pltpu.make_async_remote_copy(
            src_ref=ref, dst_ref=ref, send_sem=ss.at[hf, slot], recv_sem=rs.at[hf, slot],
            device_id=(to, head), device_id_type=MESH,
        )

    def second(buf, ss, rs, hf, dr, item, arriving):
        dist = item // 2 + 1
        sub = (0 if dr > 0 else 1) if item == 6 else item % 2
        major = mod(major0[hf] - dr * (dist if arriving else dist - 1), RING)
        ref = buf.at[hf, major, sub * 4 : sub * 4 + 4]
        to = ctx_of(hf, mod(major0[hf] + dr, RING), minor0[hf])
        way = 0 if dr > 0 else 1
        return pltpu.make_async_remote_copy(
            src_ref=ref, dst_ref=ref, send_sem=ss.at[hf, way, item], recv_sem=rs.at[hf, way, item],
            device_id=(to, head), device_id_type=MESH,
        )

    STREAMS = [(hf, dr) for hf in (0, 1) for dr in (1, -1)]
    reach = {(0, 1): 4, (0, -1): 3, (1, 1): 3, (1, -1): 4}
    w1 = functools.partial(first, w, w1_s, w1_r)
    w2 = functools.partial(second, w, w2_s, w2_r)

    def w_hop(dist):
        for hf, dr in STREAMS:
            if 0 < dist <= reach[hf, dr]:
                w1(hf, dr, dist, True).wait_recv()
            if dist < reach[hf, dr]:
                w1(hf, dr, dist + 1, False).start()

    def w_pass(item):
        for hf, dr in STREAMS:
            w2(hf, dr, item, True).wait_recv()
            if item < (5 if dr > 0 else 4):
                w2(hf, dr, min(item + 2, 6), False).start()
            elif dr < 0 and item == 5:
                w2(hf, dr, 6, False).start()

    def w_rows():
        for item in (0, 1):
            for hf, dr in STREAMS:
                w2(hf, dr, item, False).start()

    sib_kv(core, my_k).start()
    for i in (0, 1):
        sib_q(core, i).start()
    for dr in (1, -1):
        ring_kv(dr, 1, False).start()
    sib_w(core).start()
    for fetch in fetches[2:]:
        fetch.wait()

    def weigh(m, i, s, v, fresh):
        n = s.shape[1]
        top = jnp.broadcast_to(jnp.max(s, axis=1, keepdims=True) * SCALE, (TOK, ADH))
        new = top if fresh else jnp.maximum(peak[m, i], top)
        p = jnp.exp2(s * SCALE - jnp.concatenate([new] * (n // ADH), axis=1)).astype(BF)
        pv = dot(p, jnp.concatenate([v, jnp.ones((n, ADH), BF)], axis=1))
        if fresh:
            acc[m, i] = pv
        else:
            shrink = jnp.exp2(peak[m, i] - new)
            acc[m, i] = acc[m, i] * jnp.concatenate([shrink, shrink], axis=1) + pv
        peak[m, i] = new

    rows = lax.broadcasted_iota(jnp.int32, (TOK, TOK), 0)
    cols = lax.broadcasted_iota(jnp.int32, (TOK, TOK), 1)
    causal = rows >= cols

    def own_block(m, _):
        at, q = k_place(m), q_place(m)
        for i in (0, 1):
            s = jnp.where(causal, dot_nt(qs[m, q, i], kv[m, at, 0]), NEG)
            weigh(m, i, s, kv[m, at, 1], True)
        return 0

    def tile(step):
        away = jnp.where(step == 1, 1, jnp.where(step == 2, 7, jnp.where(step == 3, 2, jnp.where(step == 4, 6, 0))))
        away = jnp.where(step == 5, 4, jnp.where(step == 6, 3, jnp.where(step == 7, 5, away)))

        def one(m, _):
            q = mod(q_place(m) + away, RING)
            at_z = y + jnp.where(q > z, 1, 0)
            at_y = jnp.where(q > y, RING, jnp.where(q == y, z, 0))
            blocks = jnp.where(m == 0, at_z, at_y)

            @pl.when(step > 0)
            def _():
                acc[m] = jnp.zeros((2, TOK, 2 * ADH), F32)
                peak[m] = jnp.full((2, TOK, ADH), NEG, F32)

            def keys(t, _):
                ks = kv[m, pl.ds(2 * t, 2), 0].reshape(2 * TOK, ADH)
                vs = kv[m, pl.ds(2 * t, 2), 1].reshape(2 * TOK, ADH)
                block = 2 * t + lax.broadcasted_iota(jnp.int32, (1, 2 * TOK), 1) // TOK
                bias = jnp.where(block < blocks, 0.0, NEG)
                for i in (0, 1):
                    weigh(m, i, dot_nt(qs[m, q, i], ks) + bias, vs, False)
                return 0

            lax.fori_loop(0, (blocks + 1) // 2, keys, 0)
            for i in (0, 1):
                total = jnp.maximum(acc[m, i][:, ADH:], 1e-30)
                part_o[m, away, i] = acc[m, i][:, :ADH] / total
                part_l[m, away, i] = peak[m, i] + jnp.log2(total)
            return 0

        lax.fori_loop(0, 2, one, 0)

    small = lax.broadcasted_iota(jnp.int32, (ADH, ADH), 0) == lax.broadcasted_iota(jnp.int32, (ADH, ADH), 1)

    def packed(l):
        halves = [l[r * ADH : (r + 1) * ADH] for r in (0, 1)]
        return [jnp.sum(jnp.where(small, half, 0.0), axis=0, keepdims=True) for half in halves]

    def unpacked(block, i):
        halves = []
        for r in (0, 1):
            row = jnp.broadcast_to(block[2 * i + r : 2 * i + r + 1], (ADH, ADH))
            column = jnp.sum(jnp.where(small, row, 0.0), axis=1, keepdims=True)
            halves.append(jnp.broadcast_to(column, (ADH, ADH)))
        return jnp.concatenate(halves, axis=0)

    def join(o1, l1, o2, l2):
        top = jnp.maximum(l1, l2)
        w1_, w2_ = jnp.exp2(l1 - top), jnp.exp2(l2 - top)
        total = w1_ + w2_
        return (o1 * w1_ + o2 * w2_) / total, top + jnp.log2(total)

    def back_o(m, way, k):
        at = (m, way, k - 1) if k < 4 else (m, way, 3, way)
        to = ctx_at(m, mod(q_place(m) + (1 if way == 0 else -1), RING), k_place(m))
        return pltpu.make_async_remote_copy(
            src_ref=tx_o.at[at], dst_ref=rx_o.at[at], send_sem=o_s.at[m, way, k - 1], recv_sem=o_r.at[m, way, k - 1],
            device_id=(to, head), device_id_type=MESH,
        )

    def back_l(m, way, k):
        at = (m, way, k - 1)
        to = ctx_at(m, mod(q_place(m) + (1 if way == 0 else -1), RING), k_place(m))
        return pltpu.make_async_remote_copy(
            src_ref=tx_l.at[at], dst_ref=rx_l.at[at], send_sem=l_s.at[at], recv_sem=l_r.at[at],
            device_id=(to, head), device_id_type=MESH,
        )

    def back(k, way):
        away = k if way == 0 else RING - k

        def one(m, _):
            if k < 4:
                back_o(m, way, k + 1).wait_recv()
                back_l(m, way, k + 1).wait_recv()
            stats = []
            for i in (0, 1):
                o, l = part_o[m, away, i], part_l[m, away, i]
                if k < 3 or (k == 3 and i == way):
                    came = rx_o[m, way, k, i].astype(F32)
                    o, l = join(o, l, came, unpacked(rx_l[m, way, k], i))
                if k < 4 or i == way:
                    tx_o[m, way, k - 1, i] = o.astype(BF)
                stats += packed(l)
            tx_l[m, way, k - 1] = jnp.concatenate(stats + [jnp.zeros((4, ADH), F32)], axis=0)
            back_o(m, way, k).start()
            back_l(m, way, k).start()
            return 0

        lax.fori_loop(0, 2, one, 0)

    def collect():
        for m in (0, 1):
            for way in (0, 1):
                back_o(m, way, 1).wait_recv()
                back_l(m, way, 1).wait_recv()
            for i in (0, 1):
                o, l = part_o[m, 0, i], part_l[m, 0, i]
                for way in (0, 1):
                    came = rx_o[m, way, 0, i].astype(F32)
                    o, l = join(o, l, came, unpacked(rx_l[m, way, 0], i))
                f = 2 * m + i
                heads[:, f * ADH : (f + 1) * ADH] = o.astype(BF)

    lane = lax.broadcasted_iota(jnp.int32, (1, ADH), 1) < 64

    def tri():
        return jnp.where(causal, 1.0, 0.0).astype(F32)

    def spread(pair):
        rows2 = [jnp.broadcast_to(decay_ref[pl.ds(2 * pair + i, 1), :], (64, TOK)) for i in (0, 1)]
        return dot_nt(tri(), jnp.concatenate(rows2, axis=0), lax.Precision.HIGHEST)

    def pair_columns(pair):
        return lanes(pair, ADH)

    def split(vec):
        hi = vec.astype(BF)
        lo = (vec - hi.astype(F32)).astype(BF)
        return jnp.concatenate([jnp.broadcast_to(hi, (8, ADH)), jnp.broadcast_to(lo, (8, ADH))], axis=0)

    def joined(block):
        return block[64:65].astype(F32) + block[72:73].astype(F32)

    def row_copy(out, into, ss, rs, dz, arriving):
        there = mod(z + dz, RING)
        src = mod(z - dz, RING) if arriving else z
        return pltpu.make_async_remote_copy(
            src_ref=out.at[there], dst_ref=into.at[src], send_sem=ss.at[dz], recv_sem=rs.at[dz],
            device_id=(y * RING + there, head), device_id_type=MESH,
        )

    def column_copy(dy, arriving):
        there = mod(y + dy, RING)
        src = mod(y - dy, RING) if arriving else y
        return pltpu.make_async_remote_copy(
            src_ref=tot_out, dst_ref=tot_in.at[src], send_sem=tot_s.at[dy], recv_sem=tot_r.at[dy],
            device_id=(there * RING + z, head), device_id_type=MESH,
        )

    def every(f):
        def one(i, _):
            f(i)
            return 0

        lax.fori_loop(1, RING, one, 0)

    def states_out():
        arow[...] = dot_nt(decay_ref[...], tri(), lax.Precision.HIGHEST)
        bt = b_ref[...].astype(F32).T

        def one(pair, _):
            xp = x_ref[:, pair_columns(pair)]
            parts = []
            for i in (0, 1):
                a = arow[pl.ds(2 * pair + i, 1), :]
                tail = jnp.exp(a - a[:, TOK - 1 :]) * step_ref[pl.ds(2 * pair + i, 1), :]
                parts.append(dot((bt * tail).astype(BF), xp))
            state = jnp.where(lane, parts[0], parts[1]).astype(BF)
            last = [arow[pl.ds(2 * pair + i, 1), :][:, TOK - 1 :] for i in (0, 1)]
            through = split(jnp.exp(-jnp.where(lane, last[0], last[1])))
            for i in (0, 1):
                st_out[2 * pair + i, :64] = state[64 * i : 64 * i + 64]
                st_out[2 * pair + i, 64:] = through
            return 0

        lax.fori_loop(0, 4, one, 0)
        every(lambda dz: row_copy(st_out, st_in, st_s, st_r, dz, False).start())
        st_in[z] = st_out[z]

    def totals_out():
        every(lambda dz: row_copy(st_out, st_in, st_s, st_r, dz, True).wait_recv())

        def one(i, carry):
            state, decay = carry
            pre[i] = state
            predec[i] = jnp.broadcast_to(decay, (8, ADH))
            block = st_in[i]
            t = joined(block)
            return t * state + block[:64].astype(F32), t * decay

        state, decay = lax.fori_loop(0, RING, one, (jnp.zeros((64, ADH), F32), jnp.ones((1, ADH), F32)))
        tot_out[:64] = state.astype(BF)
        tot_out[64:] = split(decay)
        every(lambda dy: column_copy(dy, False).start())

    def incoming_out():
        every(lambda dy: column_copy(dy, True).wait_recv())

        def one(i, state):
            block = tot_in[i]
            return joined(block) * state + block[:64].astype(F32)

        state = lax.fori_loop(0, y, one, jnp.zeros((64, ADH), F32))

        def give(i, _):
            ret_out[i] = (pre[i] + predec[i][:1] * state).astype(BF)
            return 0

        lax.fori_loop(0, RING, give, 0)
        every(lambda dz: row_copy(ret_out, ret_in, ret_s, ret_r, dz, False).start())
        ret_in[z] = ret_out[z]

    def mix_pair(pair):
        if pair == 0:
            every(lambda dz: row_copy(ret_out, ret_in, ret_s, ret_r, dz, True).wait_recv())
            scores[...] = dot_nt(c_ref[...], b_ref[...])
            squares[...] = jnp.zeros_like(squares)

        at = pair_columns(pair)
        xp = x_ref[:, at]
        a_t = spread(pair)
        parts = []
        for i in (0, 1):
            a_u = arow[pl.ds(2 * pair + i, 1), :]
            gap = jnp.where(causal, a_u - a_t[:, 64 * i : 64 * i + 1], NEG)
            mixing = jnp.exp(gap) * (scores[...] * step_ref[pl.ds(2 * pair + i, 1), :])
            parts.append(dot(mixing.astype(BF), xp))
        carried = dot(c_ref[...], ret_in[pl.ds(2 * pair, 2)].reshape(ADH, ADH)) * jnp.exp(-a_t)
        skip = jnp.where(lane, skip_ref[2 * pair], skip_ref[2 * pair + 1])
        total = jnp.where(lane, parts[0], parts[1]) + carried + skip * xp.astype(F32)
        g = gate_ref[:, at].astype(F32)
        total = total * (g / (1.0 + jnp.exp(-g)))
        gated[:, at] = total
        squares[...] += jnp.broadcast_to(jnp.sum(total * total, axis=1, keepdims=True), (TOK, ADH))

    def mix_end():
        norm = lax.rsqrt(squares[...] / 512.0 + 1e-05)
        norm = jnp.concatenate([norm] * 4, axis=1)
        ssm_ref[...] = (gated[...] * norm * gain_ref[...].astype(F32)).astype(BF)

    sib_w(1 - core).wait_recv()
    w_hop(0)
    for i in (0, 1):
        sib_q(1 - core, i).wait_recv()
    kv_hop(1)
    states_out()
    kv_hop(2)
    q_hop(0)
    sib_kv(1 - core, k_place(1 - core)).wait_recv()
    lax.fori_loop(0, 2, own_block, 0)
    kv_hop(3)
    w_hop(1)
    kv_hop(4)
    totals_out()
    q_hop(1)
    w_hop(2)

    def rest(i, _):
        sib_kv(1 - core, mod(k_place(1 - core) + i, RING)).wait_recv()
        return 0

    lax.fori_loop(1, RING, rest, 0)

    def step(i, _):
        @pl.when(i == 1)
        def _():
            q_hop(2)
            w_hop(3)

        @pl.when(i == 2)
        def _():
            q_hop(3)
            w_hop(4)
            w_rows()

        @pl.when(i == 3)
        def _():
            q_hop(4)
            incoming_out()

        @pl.when(i == 5)
        def _():
            w_pass(0)

        tile(i)

        @pl.when(i == 5)
        def _():
            back(4, 0)
            back(4, 1)

        @pl.when(i == 6)
        def _():
            back(3, 0)
            w_pass(1)

        return 0

    lax.fori_loop(0, 8, step, 0)
    back(3, 1)
    mix_pair(0)
    w_pass(2)
    back(2, 0)
    back(2, 1)
    mix_pair(1)
    w_pass(3)
    back(1, 0)
    back(1, 1)
    mix_pair(2)
    w_pass(4)
    mix_pair(3)
    collect()
    w_pass(5)
    w_pass(6)

    def product(f):
        left = dot_nt(heads[:, :256], w[0, f].reshape(512, 256))
        right = dot_nt(heads[:, 256:], w[1, :, f].reshape(512, 256))
        return (left + right).astype(BF)

    def sib_copy(o):
        return pltpu.make_async_remote_copy(
            src_ref=sib_out.at[o], dst_ref=sib_in.at[o], send_sem=sib_s.at[o], recv_sem=sib_r.at[o],
            device_id=(me, 2 * xc + 1 - core), device_id_type=MESH,
        )

    def side(way):
        return (me, 2 * mod(xc + (1 if way == 0 else -1), XS) + core)

    def x1_copy(way):
        return pltpu.make_async_remote_copy(
            src_ref=x1_out.at[way], dst_ref=x1_in.at[way], send_sem=x1_s.at[way], recv_sem=x1_r.at[way],
            device_id=side(way), device_id_type=MESH,
        )

    def x2_copy(way, part):
        ref = (way, pl.ds(part * HALF, HALF))
        return pltpu.make_async_remote_copy(
            src_ref=x2_out.at[ref], dst_ref=x2_in.at[ref], send_sem=x2_s.at[way, part], recv_sem=x2_r.at[way, part],
            device_id=side(way), device_id_type=MESH,
        )

    def for_sibling(o):
        sib_out[o] = product(2 * mod(xc + o, XS) + 1 - core)
        sib_copy(o).start()

    def for_own(o):
        mine[o] = product(2 * mod(xc + o, XS) + core)

    def both(o, part):
        at = pl.ds(part * HALF, HALF)
        return mine[o, at].astype(F32) + sib_in[o, at].astype(F32)

    for_sibling(2)
    for_own(2)
    for_sibling(1)
    for_sibling(3)
    sib_copy(2).wait_recv()
    for way in (0, 1):
        x1_out[way] = both(2, way).astype(BF)
        x1_copy(way).start()
    for way, o in ((0, 1), (1, 3)):
        for_own(o)
        sib_copy(o).wait_recv()
        x2_out[way, (1 - way) * HALF : (2 - way) * HALF] = both(o, 1 - way).astype(BF)
        x2_copy(way, 1 - way).start()
    for way, o in ((0, 1), (1, 3)):
        x1_copy(way).wait_recv()
        x2_out[way, way * HALF : (way + 1) * HALF] = (both(o, way) + x1_in[way].astype(F32)).astype(BF)
        x2_copy(way, way).start()
    for_sibling(0)
    for_own(0)
    mix_end()
    sib_copy(0).wait_recv()
    for part in (1, 0):
        x2_copy(0, part).wait_recv()
        x2_copy(1, part).wait_recv()
    for part in (0, 1):
        at = pl.ds(part * HALF, HALF)
        out_ref[at] = (both(0, part) + x2_in[0, at].astype(F32) + x2_in[1, at].astype(F32)).astype(BF)

    def sent(i, _):
        sib_kv(core, i).wait_send()
        return 0

    lax.fori_loop(0, RING, sent, 0)
    for i in (0, 1):
        sib_q(core, i).wait_send()
    sib_w(core).wait_send()
    for dist in range(1, 5):
        for dr in (1, -1):
            ring_kv(dr, dist, False).wait_send()

    def sent_both(m, _):
        for k in range(1, 5):
            for way, dr in ((0, 1), (1, -1)):
                ring_q(m, dr, k, False).wait_send()
                back_o(m, way, k).wait_send()
                back_l(m, way, k).wait_send()
        return 0

    lax.fori_loop(0, 2, sent_both, 0)
    for hf, dr in STREAMS:
        for dist in range(1, reach[hf, dr] + 1):
            w1(hf, dr, dist, False).wait_send()
        for item in range(7):
            w2(hf, dr, item, False).wait_send()
    every(lambda d: row_copy(st_out, st_in, st_s, st_r, d, False).wait_send())
    every(lambda d: column_copy(d, False).wait_send())
    every(lambda d: row_copy(ret_out, ret_in, ret_s, ret_r, d, False).wait_send())
    for o in range(4):
        sib_copy(o).wait_send()
    for way in (0, 1):
        x1_copy(way).wait_send()
        for part in (0, 1):
            x2_copy(way, part).wait_send()


def per_device(
    x_in, gate_z, b_in, c_in, step_size, log_decay, d_skip, norm_gain, query, key, value, o_weight
):
    vmem = pl.BlockSpec(memory_space=pltpu.VMEM)
    smem = pl.BlockSpec(memory_space=pltpu.SMEM)
    hbm = pl.BlockSpec(memory_space=pl.ANY)
    dma = pltpu.SemaphoreType.DMA
    tokens = (TOK, 512)
    return pl.pallas_call(
        kernel,
        out_shape=(jax.ShapeDtypeStruct(tokens, BF), jax.ShapeDtypeStruct(tokens, BF)),
        in_specs=[hbm] * 6 + [smem, vmem] + [hbm] * 4,
        out_specs=(vmem, vmem),
        scratch_shapes=[
            pltpu.VMEM(tokens, BF),
            pltpu.VMEM(tokens, BF),
            pltpu.VMEM((TOK, ADH), BF),
            pltpu.VMEM((TOK, ADH), BF),
            pltpu.VMEM((8, TOK), F32),
            pltpu.VMEM((8, TOK), F32),
            pltpu.VMEM((2, RING, 2, TOK, ADH), BF),
            pltpu.VMEM((2, RING, 2, TOK, ADH), BF),
            pltpu.VMEM((2, RING, RING, 64, 256), BF),
            pltpu.VMEM((2, 2, TOK, 2 * ADH), F32),
            pltpu.VMEM((2, 2, TOK, ADH), F32),
            pltpu.VMEM((2, RING, 2, TOK, ADH), F32),
            pltpu.VMEM((2, RING, 2, TOK, ADH), F32),
            pltpu.VMEM((2, 2, 4, 2, TOK, ADH), BF),
            pltpu.VMEM((2, 2, 4, 8, ADH), F32),
            pltpu.VMEM((2, 2, 4, 2, TOK, ADH), BF),
            pltpu.VMEM((2, 2, 4, 8, ADH), F32),
            pltpu.VMEM(tokens, BF),
            pltpu.VMEM((8, TOK), F32),
            pltpu.VMEM((TOK, TOK), F32),
            pltpu.VMEM(tokens, F32),
            pltpu.VMEM((TOK, ADH), F32),
            pltpu.VMEM((RING, 80, ADH), BF),
            pltpu.VMEM((RING, 80, ADH), BF),
            pltpu.VMEM((RING, 64, ADH), F32),
            pltpu.VMEM((RING, 8, ADH), F32),
            pltpu.VMEM((80, ADH), BF),
            pltpu.VMEM((RING, 80, ADH), BF),
            pltpu.VMEM((RING, 64, ADH), BF),
            pltpu.VMEM((RING, 64, ADH), BF),
            pltpu.VMEM((XS,) + tokens, BF),
            pltpu.VMEM((XS,) + tokens, BF),
            pltpu.VMEM((XS,) + tokens, BF),
            pltpu.VMEM((2, HALF, 512), BF),
            pltpu.VMEM((2, HALF, 512), BF),
            pltpu.VMEM((2,) + tokens, BF),
            pltpu.VMEM((2,) + tokens, BF),
            dma((11,)), dma((8,)), dma((8,)), dma((2,)), dma((2,)), dma, dma, dma((2, 4)), dma((2, 4)),
            dma((2, 2, 4)), dma((2, 2, 4)), dma((2, 2, 4)), dma((2, 2, 4)), dma((2, 2, 4)), dma((2, 2, 4)),
            dma((2, 8)), dma((2, 8)), dma((2, 2, 7)), dma((2, 2, 7)),
            dma((8,)), dma((8,)), dma((8,)), dma((8,)), dma((8,)), dma((8,)),
            dma((4,)), dma((4,)), dma((2,)), dma((2,)), dma((2, 2)), dma((2, 2)),
        ],
        compiler_params=pltpu.CompilerParams(
            collective_id=0, has_side_effects=True, vmem_limit_bytes=60 * 1024 * 1024
        ),
        name="mixer_and_attention",
    )(
        x_in, gate_z, b_in, c_in, step_size, log_decay, d_skip, norm_gain.reshape(1, 512),
        query, key, value, o_weight.T,
    )


def solution(mesh):
    in_specs = (
        P("ctx", "head"),
        P("ctx", "head"),
        P("ctx", "head"),
        P("ctx", "head"),
        P("head", "ctx"),
        P("head", "ctx"),
        P("head"),
        P("head"),
        P("ctx", "head"),
        P("ctx", "head"),
        P("ctx", "head"),
        P("head", "ctx"),
    )
    out_specs = (P("ctx", "head"), P("ctx", "head"))
    return jax.shard_map(
        per_device, mesh=mesh, in_specs=in_specs, out_specs=out_specs, check_vma=False
    )
```

time: 135 us -> 114 us (0.84)
  Pallas kernels: 122 us -> 109 us
  local copies, waits for them, and re-layouts: 11.2 us -> 3.67 us
    pallas_call x1, Pallas kernels: 122 us -> 109 us  [per_device(): pl.pallas_call(kernel, out_shape=(jax.ShapeDtypeStruct(tokens, BF), jax.S...]
    unnamed x26 -> x6, local copies, waits for them, and re-layouts: 11.2 us -> 3.09 us
where the time goes in v2:
time: 114 us
  Pallas kernels  109 us (96%)
  local copies, waits for them, and re-layouts  3.67 us (3%)
    pallas_call x1, Pallas kernels, per_device(): pl.pallas_call(kernel, out_shape=(jax.ShapeDtypeStruct(tokens, BF), jax.S...  109 us
    unnamed x6, local copies, waits for them, and re-layouts  3.09 us

profile of v2, /device:TPU:1, one launch (start us, length us, event | category | flops | bytes accessed | tf_op | source)
XLA Modules:
  0.0 113.8 jit_solution(10103430642975862929)
XLA Ops:
  0.6 0.0 copy-start.1
  0.6 0.7 copy-done.1
  1.3 0.6 reshape.7.gain_ref
  1.9 109.5 %mixer_and_attention.1 = (bf16[256,512]{1,0:T(8,128)(2,1)}, bf16[256,512]{1,0:T(8,128)(2,1)}) custom-call(bf16[256,512]{1,0:T(8,128)(2,1)} %x_hbm.1, bf16[256,512]{1,0:T(8,128)(2,1)} %gate_hbm.1, bf16[256,128]{1,0:T(8,128)(2,1)} %b_hbm.1, bf16[256,128]{1,0:T(8,128)(2,1)} %c_hbm.1, f32[8,256]{1,0:T(8,128)} %step_hbm.1, f32[8,256]{1,0:T(8,128)} %decay_hbm.1, ...), custom_call_target="tpu_custom_call" | custom-call | tf_op jit(solution)/shard_map/mixer_and_attention/pallas_call | solution.py:656
  111.4 0.0 copy-start
  111.4 1.7 %copy.16 = bf16[256,512]{1,0:T(8,128)(2,1)} copy(bf16[256,512]{1,0:T(8,128)(2,1)} %get-tuple-element.4) | data formatting | bytes 524288
  113.1 0.0 copy-done
  113.1 0.7 copy.17
Async XLA Ops:
  0.6 0.7 copy-start.1
  111.4 1.7 %copy-start = (bf16[256,512]{1,0:T(8,128)(2,1)S(1)}, bf16[256,512]{1,0:T(8,128)(2,1)}, u32[]{:S(2)}) copy-start(bf16[256,512]{1,0:T(8,128)(2,1)} %get-tuple-element.5) | copy-start | bytes 786436

commit v3 on v2

--- a/solution.py
+++ b/solution.py
@@ -118,42 +118,49 @@
             send_sem=sw_s, recv_sem=sw_r, device_id=sibling, device_id_type=MESH,
         )
 
-    def ring_kv(dr, dist, arriving):
+    def ring_kv(dr, dist, part, arriving):
         way = 0 if dr > 0 else 1
         place = mod(my_k - dr * (dist if arriving else dist - 1), RING)
-        ref = kv.at[core, place] if dist < 4 else kv.at[core, place, way]
+        ref = kv.at[core, place, part]
         to = ctx_at(core, my_q, mod(my_k + dr, RING))
-        return pltpu.make_async_remote_copy(
-            src_ref=ref, dst_ref=ref, send_sem=kr_s.at[way, dist - 1], recv_sem=kr_r.at[way, dist - 1],
+        at = (way, dist - 1, part)
+        return pltpu.make_async_remote_copy(
+            src_ref=ref, dst_ref=ref, send_sem=kr_s.at[at], recv_sem=kr_r.at[at],
             device_id=(to, head), device_id_type=MESH,
         )
 
-    def ring_q(m, dr, dist, arriving):
+    def ring_q(m, dr, dist, part, arriving):
         way = 0 if dr > 0 else 1
         place = mod(q_place(m) - dr * (dist if arriving else dist - 1), RING)
-        ref = qs.at[m, place] if dist < 4 else qs.at[m, place, way]
+        ref = qs.at[m, place, part]
         to = ctx_at(m, mod(q_place(m) + dr, RING), k_place(m))
-        return pltpu.make_async_remote_copy(
-            src_ref=ref, dst_ref=ref, send_sem=qr_s.at[m, way, dist - 1], recv_sem=qr_r.at[m, way, dist - 1],
+        at = (m, way, dist - 1, part)
+        return pltpu.make_async_remote_copy(
+            src_ref=ref, dst_ref=ref, send_sem=qr_s.at[at], recv_sem=qr_r.at[at],
             device_id=(to, head), device_id_type=MESH,
         )
 
+    def goes(dr, dist, part):
+        return dist < 4 or (dist == 4 and part == (0 if dr > 0 else 1))
+
     def kv_hop(dist):
-        for dr in (1, -1):
-            ring_kv(dr, dist, True).wait_recv()
-            if dist < 4:
-                ring_kv(dr, dist + 1, False).start()
+        for part in (0, 1):
+            for dr in (1, -1):
+                if dist > 0 and goes(dr, dist, part):
+                    ring_kv(dr, dist, part, True).wait_recv()
+                if goes(dr, dist + 1, part):
+                    ring_kv(dr, dist + 1, part, False).start()
+        if dist > 0:
+            for dr in (1, -1) if dist < 4 else (1,):
                 sib_kv(core, mod(my_k - dr * dist, RING)).start()
-        if dist == 4:
-            sib_kv(core, mod(my_k + 4, RING)).start()
-
-    def q_hop(dist):
+
+    def q_hop(dist, part):
         for m in (0, 1):
             for dr in (1, -1):
-                if dist > 0:
-                    ring_q(m, dr, dist, True).wait_recv()
-                if dist < 4:
-                    ring_q(m, dr, dist + 1, False).start()
+                if dist > 0 and goes(dr, dist, part):
+                    ring_q(m, dr, dist, part, True).wait_recv()
+                if goes(dr, dist + 1, part):
+                    ring_q(m, dr, dist + 1, part, False).start()
 
     def first(buf, ss, rs, hf, dr, dist, arriving):
         slot = dist - 1 + (0 if dr > 0 else 4)
@@ -165,15 +172,15 @@
             device_id=(to, head), device_id_type=MESH,
         )
 
-    def second(buf, ss, rs, hf, dr, item, arriving):
-        dist = item // 2 + 1
-        sub = (0 if dr > 0 else 1) if item == 6 else item % 2
+    def second(buf, ss, rs, hf, dr, dist, pair, arriving):
+        way = 0 if dr > 0 else 1
         major = mod(major0[hf] - dr * (dist if arriving else dist - 1), RING)
-        ref = buf.at[hf, major, sub * 4 : sub * 4 + 4]
+        two = mod(minor0[hf] // 2 + (0, 1, 3, 2)[pair], RING // 2)
+        ref = buf.at[hf, major, pl.ds(2 * two, 2)]
         to = ctx_of(hf, mod(major0[hf] + dr, RING), minor0[hf])
-        way = 0 if dr > 0 else 1
-        return pltpu.make_async_remote_copy(
-            src_ref=ref, dst_ref=ref, send_sem=ss.at[hf, way, item], recv_sem=rs.at[hf, way, item],
+        at = (hf, way, dist - 1, pair)
+        return pltpu.make_async_remote_copy(
+            src_ref=ref, dst_ref=ref, send_sem=ss.at[at], recv_sem=rs.at[at],
             device_id=(to, head), device_id_type=MESH,
         )
 
@@ -189,26 +196,22 @@
             if dist < reach[hf, dr]:
                 w1(hf, dr, dist + 1, False).start()
 
-    def w_pass(item):
+    def w_goes(dr, dist, pair):
+        return dist < 4 or (dist == 4 and (pair < 2) == (dr > 0))
+
+    def w_pass(dist, pair):
         for hf, dr in STREAMS:
-            w2(hf, dr, item, True).wait_recv()
-            if item < (5 if dr > 0 else 4):
-                w2(hf, dr, min(item + 2, 6), False).start()
-            elif dr < 0 and item == 5:
-                w2(hf, dr, 6, False).start()
-
-    def w_rows():
-        for item in (0, 1):
-            for hf, dr in STREAMS:
-                w2(hf, dr, item, False).start()
-
+            if dist > 0 and w_goes(dr, dist, pair):
+                w2(hf, dr, dist, pair, True).wait_recv()
+            if w_goes(dr, dist + 1, pair):
+                w2(hf, dr, dist + 1, pair, False).start()
+
+    kv_hop(0)
     sib_kv(core, my_k).start()
     for i in (0, 1):
         sib_q(core, i).start()
-    for dr in (1, -1):
-        ring_kv(dr, 1, False).start()
     sib_w(core).start()
-    for fetch in fetches[2:]:
+    for fetch in fetches[2:5]:
         fetch.wait()
 
     def weigh(m, i, s, v, fresh):
@@ -232,12 +235,12 @@
         at, q = k_place(m), q_place(m)
         for i in (0, 1):
             s = jnp.where(causal, dot_nt(qs[m, q, i], kv[m, at, 0]), NEG)
-            weigh(m, i, s, kv[m, at, 1], True)
+            weigh(2 + m, i, s, kv[m, at, 1], True)
         return 0
 
     def tile(step):
-        away = jnp.where(step == 1, 1, jnp.where(step == 2, 7, jnp.where(step == 3, 2, jnp.where(step == 4, 6, 0))))
-        away = jnp.where(step == 5, 4, jnp.where(step == 6, 3, jnp.where(step == 7, 5, away)))
+        near_by = 4 - (step + 1) // 2
+        away = jnp.where(step % 2 == 1, near_by, mod(RING - near_by, RING))
 
         def one(m, _):
             q = mod(q_place(m) + away, RING)
@@ -245,7 +248,9 @@
             at_y = jnp.where(q > y, RING, jnp.where(q == y, z, 0))
             blocks = jnp.where(m == 0, at_z, at_y)
 
-            @pl.when(step > 0)
+            t_at = jnp.where(step == 7, 2 + m, m)
+
+            @pl.when(step < 7)
             def _():
                 acc[m] = jnp.zeros((2, TOK, 2 * ADH), F32)
                 peak[m] = jnp.full((2, TOK, ADH), NEG, F32)
@@ -253,17 +258,24 @@
             def keys(t, _):
                 ks = kv[m, pl.ds(2 * t, 2), 0].reshape(2 * TOK, ADH)
                 vs = kv[m, pl.ds(2 * t, 2), 1].reshape(2 * TOK, ADH)
-                block = 2 * t + lax.broadcasted_iota(jnp.int32, (1, 2 * TOK), 1) // TOK
-                bias = jnp.where(block < blocks, 0.0, NEG)
+                both = [dot_nt(qs[m, q, i], ks) for i in (0, 1)]
                 for i in (0, 1):
-                    weigh(m, i, dot_nt(qs[m, q, i], ks) + bias, vs, False)
+                    weigh(t_at, i, both[i], vs, False)
                 return 0
 
-            lax.fori_loop(0, (blocks + 1) // 2, keys, 0)
+            lax.fori_loop(0, blocks // 2, keys, 0)
+
+            @pl.when(blocks % 2 == 1)
+            def _():
+                ks, vs = kv[m, blocks - 1, 0], kv[m, blocks - 1, 1]
+                both = [dot_nt(qs[m, q, i], ks) for i in (0, 1)]
+                for i in (0, 1):
+                    weigh(t_at, i, both[i], vs, False)
+
             for i in (0, 1):
-                total = jnp.maximum(acc[m, i][:, ADH:], 1e-30)
-                part_o[m, away, i] = acc[m, i][:, :ADH] / total
-                part_l[m, away, i] = peak[m, i] + jnp.log2(total)
+                total = jnp.maximum(acc[t_at, i][:, ADH:], 1e-30)
+                part_o[m, away, i] = acc[t_at, i][:, :ADH] / total
+                part_l[m, away, i] = peak[t_at, i] + jnp.log2(total)
             return 0
 
         lax.fori_loop(0, 2, one, 0)
@@ -274,10 +286,10 @@
         halves = [l[r * ADH : (r + 1) * ADH] for r in (0, 1)]
         return [jnp.sum(jnp.where(small, half, 0.0), axis=0, keepdims=True) for half in halves]
 
-    def unpacked(block, i):
+    def unpacked(block):
         halves = []
         for r in (0, 1):
-            row = jnp.broadcast_to(block[2 * i + r : 2 * i + r + 1], (ADH, ADH))
+            row = jnp.broadcast_to(block[r : r + 1], (ADH, ADH))
             column = jnp.sum(jnp.where(small, row, 0.0), axis=1, keepdims=True)
             halves.append(jnp.broadcast_to(column, (ADH, ADH)))
         return jnp.concatenate(halves, axis=0)
@@ -288,55 +300,43 @@
         total = w1_ + w2_
         return (o1 * w1_ + o2 * w2_) / total, top + jnp.log2(total)
 
-    def back_o(m, way, k):
-        at = (m, way, k - 1) if k < 4 else (m, way, 3, way)
+    def back_copies(m, way, k, i):
+        at = (m, way, k - 1, i)
         to = ctx_at(m, mod(q_place(m) + (1 if way == 0 else -1), RING), k_place(m))
-        return pltpu.make_async_remote_copy(
-            src_ref=tx_o.at[at], dst_ref=rx_o.at[at], send_sem=o_s.at[m, way, k - 1], recv_sem=o_r.at[m, way, k - 1],
-            device_id=(to, head), device_id_type=MESH,
-        )
-
-    def back_l(m, way, k):
-        at = (m, way, k - 1)
-        to = ctx_at(m, mod(q_place(m) + (1 if way == 0 else -1), RING), k_place(m))
-        return pltpu.make_async_remote_copy(
-            src_ref=tx_l.at[at], dst_ref=rx_l.at[at], send_sem=l_s.at[at], recv_sem=l_r.at[at],
-            device_id=(to, head), device_id_type=MESH,
-        )
-
-    def back(k, way):
+        return [
+            pltpu.make_async_remote_copy(
+                src_ref=out.at[at], dst_ref=into.at[at], send_sem=ss.at[at], recv_sem=rs.at[at],
+                device_id=(to, head), device_id_type=MESH,
+            )
+            for out, into, ss, rs in ((tx_o, rx_o, o_s, o_r), (tx_l, rx_l, l_s, l_r))
+        ]
+
+    def came(m, way, k, i):
+        for copy in back_copies(m, way, k, i):
+            copy.wait_recv()
+        return rx_o[m, way, k - 1, i].astype(F32), unpacked(rx_l[m, way, k - 1, i])
+
+    def back(k, way, i):
         away = k if way == 0 else RING - k
 
         def one(m, _):
-            if k < 4:
-                back_o(m, way, k + 1).wait_recv()
-                back_l(m, way, k + 1).wait_recv()
-            stats = []
-            for i in (0, 1):
-                o, l = part_o[m, away, i], part_l[m, away, i]
-                if k < 3 or (k == 3 and i == way):
-                    came = rx_o[m, way, k, i].astype(F32)
-                    o, l = join(o, l, came, unpacked(rx_l[m, way, k], i))
-                if k < 4 or i == way:
-                    tx_o[m, way, k - 1, i] = o.astype(BF)
-                stats += packed(l)
-            tx_l[m, way, k - 1] = jnp.concatenate(stats + [jnp.zeros((4, ADH), F32)], axis=0)
-            back_o(m, way, k).start()
-            back_l(m, way, k).start()
+            o, l = part_o[m, away, i], part_l[m, away, i]
+            if k < 3 or (k == 3 and i == way):
+                o, l = join(o, l, *came(m, way, k + 1, i))
+            tx_o[m, way, k - 1, i] = o.astype(BF)
+            tx_l[m, way, k - 1, i] = jnp.concatenate(packed(l) + [jnp.zeros((6, ADH), F32)], axis=0)
+            for copy in back_copies(m, way, k, i):
+                copy.start()
             return 0
 
         lax.fori_loop(0, 2, one, 0)
 
     def collect():
-        for m in (0, 1):
-            for way in (0, 1):
-                back_o(m, way, 1).wait_recv()
-                back_l(m, way, 1).wait_recv()
-            for i in (0, 1):
+        for i in (0, 1):
+            for m in (0, 1):
                 o, l = part_o[m, 0, i], part_l[m, 0, i]
                 for way in (0, 1):
-                    came = rx_o[m, way, 0, i].astype(F32)
-                    o, l = join(o, l, came, unpacked(rx_l[m, way, 0], i))
+                    o, l = join(o, l, *came(m, way, 1, i))
                 f = 2 * m + i
                 heads[:, f * ADH : (f + 1) * ADH] = o.astype(BF)
 
@@ -403,7 +403,6 @@
             return 0
 
         lax.fori_loop(0, 4, one, 0)
-        every(lambda dz: row_copy(st_out, st_in, st_s, st_r, dz, False).start())
         st_in[z] = st_out[z]
 
     def totals_out():
@@ -467,22 +466,35 @@
         norm = jnp.concatenate([norm] * 4, axis=1)
         ssm_ref[...] = (gated[...] * norm * gain_ref[...].astype(F32)).astype(BF)
 
+    for i in (0, 1):
+        sib_q(1 - core, i).wait_recv()
+        if i == 1:
+            for fetch in fetches[5:]:
+                fetch.wait()
+            states_out()
+        q_hop(0, i)
     sib_w(1 - core).wait_recv()
     w_hop(0)
-    for i in (0, 1):
-        sib_q(1 - core, i).wait_recv()
     kv_hop(1)
-    states_out()
-    kv_hop(2)
-    q_hop(0)
+    q_hop(1, 0)
+    every(lambda dz: row_copy(st_out, st_in, st_s, st_r, dz, False).start())
     sib_kv(1 - core, k_place(1 - core)).wait_recv()
     lax.fori_loop(0, 2, own_block, 0)
-    kv_hop(3)
+    q_hop(1, 1)
     w_hop(1)
-    kv_hop(4)
-    totals_out()
-    q_hop(1)
-    w_hop(2)
+    w_pass(0, 0)
+    for dist in (2, 3, 4):
+        kv_hop(dist)
+        q_hop(dist, 0)
+        q_hop(dist, 1)
+        w_hop(dist)
+        if dist == 3:
+            w_pass(0, 1)
+            w_pass(0, 2)
+            w_pass(1, 0)
+            totals_out()
+    w_pass(0, 3)
+    w_pass(2, 0)
 
     def rest(i, _):
         sib_kv(1 - core, mod(k_place(1 - core) + i, RING)).wait_recv()
@@ -490,57 +502,40 @@
 
     lax.fori_loop(1, RING, rest, 0)
 
+    TURNS = (
+        (), ((1, 1),), ((1, 2), (1, 3)), ((3, 0), (2, 1)),
+        ((2, 2), (2, 3)), ((4, 0), (3, 1)), ((3, 2), (3, 3)), ((4, 1), (4, 2)),
+    )
+
     def step(i, _):
-        @pl.when(i == 1)
+        for at, turns in enumerate(TURNS):
+
+            @pl.when(i == at)
+            def _(turns=turns):
+                for turn in turns:
+                    w_pass(*turn)
+
+        pl.when(i == 1)(incoming_out)
+        tile(i)
+
+        @pl.when(i == 0)
         def _():
-            q_hop(2)
-            w_hop(3)
-
-        @pl.when(i == 2)
-        def _():
-            q_hop(3)
-            w_hop(4)
-            w_rows()
-
-        @pl.when(i == 3)
-        def _():
-            q_hop(4)
-            incoming_out()
-
-        @pl.when(i == 5)
-        def _():
-            w_pass(0)
-
-        tile(i)
-
-        @pl.when(i == 5)
-        def _():
-            back(4, 0)
-            back(4, 1)
-
-        @pl.when(i == 6)
-        def _():
-            back(3, 0)
-            w_pass(1)
+            back(4, 0, 0)
+            back(4, 1, 1)
+
+        for k in (3, 2, 1):
+            for way in (0, 1):
+
+                @pl.when(i == 7 - 2 * k + way)
+                def _(k=k, way=way):
+                    back(k, way, 1 - way)
+                    back(k, way, way)
 
         return 0
 
     lax.fori_loop(0, 8, step, 0)
-    back(3, 1)
-    mix_pair(0)
-    w_pass(2)
-    back(2, 0)
-    back(2, 1)
-    mix_pair(1)
-    w_pass(3)
-    back(1, 0)
-    back(1, 1)
-    mix_pair(2)
-    w_pass(4)
-    mix_pair(3)
     collect()
-    w_pass(5)
-    w_pass(6)
+    w_pass(4, 3)
 
     def product(f):
         left = dot_nt(heads[:, :256], w[0, f].reshape(512, 256))
@@ -593,12 +588,16 @@
         sib_copy(o).wait_recv()
         x2_out[way, (1 - way) * HALF : (2 - way) * HALF] = both(o, 1 - way).astype(BF)
         x2_copy(way, 1 - way).start()
+    mix_pair(0)
+    mix_pair(1)
     for way, o in ((0, 1), (1, 3)):
         x1_copy(way).wait_recv()
         x2_out[way, way * HALF : (way + 1) * HALF] = (both(o, way) + x1_in[way].astype(F32)).astype(BF)
         x2_copy(way, way).start()
     for_sibling(0)
     for_own(0)
+    mix_pair(2)
+    mix_pair(3)
     mix_end()
     sib_copy(0).wait_recv()
     for part in (1, 0):
@@ -616,24 +615,30 @@
     for i in (0, 1):
         sib_q(core, i).wait_send()
     sib_w(core).wait_send()
-    for dist in range(1, 5):
-        for dr in (1, -1):
-            ring_kv(dr, dist, False).wait_send()
+    for k in range(1, 5):
+        for way, dr in ((0, 1), (1, -1)):
+            for part in (0, 1):
+                if goes(dr, k, part):
+                    ring_kv(dr, k, part, False).wait_send()
 
     def sent_both(m, _):
         for k in range(1, 5):
             for way, dr in ((0, 1), (1, -1)):
-                ring_q(m, dr, k, False).wait_send()
-                back_o(m, way, k).wait_send()
-                back_l(m, way, k).wait_send()
+                for part in (0, 1):
+                    if goes(dr, k, part):
+                        ring_q(m, dr, k, part, False).wait_send()
+                        for copy in back_copies(m, way, k, part):
+                            copy.wait_send()
         return 0
 
     lax.fori_loop(0, 2, sent_both, 0)
     for hf, dr in STREAMS:
         for dist in range(1, reach[hf, dr] + 1):
             w1(hf, dr, dist, False).wait_send()
-        for item in range(7):
-            w2(hf, dr, item, False).wait_send()
+        for dist in range(1, 5):
+            for pair in range(4):
+                if w_goes(dr, dist, pair):
+                    w2(hf, dr, dist, pair, False).wait_send()
     every(lambda d: row_copy(st_out, st_in, st_s, st_r, d, False).wait_send())
     every(lambda d: column_copy(d, False).wait_send())
     every(lambda d: row_copy(ret_out, ret_in, ret_s, ret_r, d, False).wait_send())
@@ -668,14 +673,14 @@
             pltpu.VMEM((2, RING, 2, TOK, ADH), BF),
             pltpu.VMEM((2, RING, 2, TOK, ADH), BF),
             pltpu.VMEM((2, RING, RING, 64, 256), BF),
-            pltpu.VMEM((2, 2, TOK, 2 * ADH), F32),
-            pltpu.VMEM((2, 2, TOK, ADH), F32),
+            pltpu.VMEM((4, 2, TOK, 2 * ADH), F32),
+            pltpu.VMEM((4, 2, TOK, ADH), F32),
             pltpu.VMEM((2, RING, 2, TOK, ADH), F32),
             pltpu.VMEM((2, RING, 2, TOK, ADH), F32),
             pltpu.VMEM((2, 2, 4, 2, TOK, ADH), BF),
-            pltpu.VMEM((2, 2, 4, 8, ADH), F32),
+            pltpu.VMEM((2, 2, 4, 2, 8, ADH), F32),
             pltpu.VMEM((2, 2, 4, 2, TOK, ADH), BF),
-            pltpu.VMEM((2, 2, 4, 8, ADH), F32),
+            pltpu.VMEM((2, 2, 4, 2, 8, ADH), F32),
             pltpu.VMEM(tokens, BF),
             pltpu.VMEM((8, TOK), F32),
             pltpu.VMEM((TOK, TOK), F32),
@@ -696,9 +701,9 @@
             pltpu.VMEM((2, HALF, 512), BF),
             pltpu.VMEM((2,) + tokens, BF),
             pltpu.VMEM((2,) + tokens, BF),
-            dma((11,)), dma((8,)), dma((8,)), dma((2,)), dma((2,)), dma, dma, dma((2, 4)), dma((2, 4)),
-            dma((2, 2, 4)), dma((2, 2, 4)), dma((2, 2, 4)), dma((2, 2, 4)), dma((2, 2, 4)), dma((2, 2, 4)),
-            dma((2, 8)), dma((2, 8)), dma((2, 2, 7)), dma((2, 2, 7)),
+            dma((11,)), dma((8,)), dma((8,)), dma((2,)), dma((2,)), dma, dma, dma((2, 4, 2)), dma((2, 4, 2)),
+            *[dma((2, 2, 4, 2))] * 6,
+            dma((2, 8)), dma((2, 8)), dma((2, 2, 4, 4)), dma((2, 2, 4, 4)),
             dma((8,)), dma((8,)), dma((8,)), dma((8,)), dma((8,)), dma((8,)),
             dma((4,)), dma((4,)), dma((2,)), dma((2,)), dma((2, 2)), dma((2, 2)),
         ],

time: 114 us -> 101 us (0.89)
  Pallas kernels: 109 us -> 96.6 us
    pallas_call x1, Pallas kernels: 109 us -> 96.6 us  [per_device(): pl.pallas_call(kernel, out_shape=(jax.ShapeDtypeStruct(tokens, BF), jax.S...]
where the time goes in v3:
time: 101 us
  Pallas kernels  96.6 us (96%)
  local copies, waits for them, and re-layouts  3.67 us (4%)
    pallas_call x1, Pallas kernels, per_device(): pl.pallas_call(kernel, out_shape=(jax.ShapeDtypeStruct(tokens, BF), jax.S...  96.6 us
    unnamed x6, local copies, waits for them, and re-layouts  3.09 us

profile of v3, /device:TPU:1, one launch (start us, length us, event | category | flops | bytes accessed | tf_op | source)
XLA Modules:
  0.0 100.9 jit_solution(4475319810378987749)
XLA Ops:
  0.6 0.0 copy-start.1
  0.6 0.7 copy-done.1
  1.3 0.6 reshape.7.gain_ref
  1.9 96.6 %mixer_and_attention.1 = (bf16[256,512]{1,0:T(8,128)(2,1)}, bf16[256,512]{1,0:T(8,128)(2,1)}) custom-call(bf16[256,512]{1,0:T(8,128)(2,1)} %x_hbm.1, bf16[256,512]{1,0:T(8,128)(2,1)} %gate_hbm.1, bf16[256,128]{1,0:T(8,128)(2,1)} %b_hbm.1, bf16[256,128]{1,0:T(8,128)(2,1)} %c_hbm.1, f32[8,256]{1,0:T(8,128)} %step_hbm.1, f32[8,256]{1,0:T(8,128)} %decay_hbm.1, ...), custom_call_target="tpu_custom_call" | custom-call | tf_op jit(solution)/shard_map/mixer_and_attention/pallas_call | solution.py:661
  98.5 0.0 copy-start
  98.5 1.7 %copy.16 = bf16[256,512]{1,0:T(8,128)(2,1)} copy(bf16[256,512]{1,0:T(8,128)(2,1)} %get-tuple-element.4) | data formatting | bytes 524288
  100.2 0.0 copy-done
  100.2 0.7 copy.17
Async XLA Ops:
  0.6 0.7 copy-start.1
  98.5 1.7 %copy-start = (bf16[256,512]{1,0:T(8,128)(2,1)S(1)}, bf16[256,512]{1,0:T(8,128)(2,1)}, u32[]{:S(2)}) copy-start(bf16[256,512]{1,0:T(8,128)(2,1)} %get-tuple-element.5) | copy-start | bytes 786436

commit v4 on v3

--- a/solution.py
+++ b/solution.py
@@ -35,9 +35,9 @@
 
 
 def kernel(
-    x_hbm, gate_hbm, b_hbm, c_hbm, step_hbm, decay_hbm, skip_ref, gain_ref, q_hbm, k_hbm, v_hbm, wt_hbm,
+    x_hbm, gate_hbm, b_hbm, c_hbm, step_hbm, decay_hbm, skip_hbm, gain_ref, q_hbm, k_hbm, v_hbm, wt_hbm,
     ssm_ref, out_ref,
-    x_ref, gate_ref, b_ref, c_ref, step_ref, decay_ref,
+    x_ref, gate_ref, b_ref, c_ref, step_ref, decay_ref, skip_ref,
     kv, qs, w, acc, peak, part_o, part_l, tx_o, tx_l, rx_o, rx_l, heads,
     arow, scores, gated, squares, st_out, st_in, pre, predec, tot_out, tot_in, ret_out, ret_in,
     sib_out, sib_in, mine, x1_out, x1_in, x2_out, x2_in,
@@ -91,12 +91,11 @@
         (step_hbm, step_ref),
         (c_hbm, c_ref),
         (gate_hbm, gate_ref),
+        (skip_hbm, skip_ref),
     ]
     fetches = [pltpu.make_async_copy(src, dst, in_s.at[i]) for i, (src, dst) in enumerate(fetches)]
     for fetch in fetches:
         fetch.start()
-    for fetch in fetches[:2]:
-        fetch.wait()
     pl.semaphore_wait(barrier, 21)
 
     def sib_kv(m, place):
@@ -124,8 +123,9 @@
         ref = kv.at[core, place, part]
         to = ctx_at(core, my_q, mod(my_k + dr, RING))
         at = (way, dist - 1, part)
-        return pltpu.make_async_remote_copy(
-            src_ref=ref, dst_ref=ref, send_sem=kr_s.at[at], recv_sem=kr_r.at[at],
+        src = (k_hbm, v_hbm)[part] if dist == 1 and not arriving else ref
+        return pltpu.make_async_remote_copy(
+            src_ref=src, dst_ref=ref, send_sem=kr_s.at[at], recv_sem=kr_r.at[at],
             device_id=(to, head), device_id_type=MESH,
         )
 
@@ -207,9 +207,11 @@
                 w2(hf, dr, dist + 1, pair, False).start()
 
     kv_hop(0)
-    sib_kv(core, my_k).start()
     for i in (0, 1):
         sib_q(core, i).start()
+    for fetch in fetches[:2]:
+        fetch.wait()
+    sib_kv(core, my_k).start()
     sib_w(core).start()
     for fetch in fetches[2:5]:
         fetch.wait()
@@ -382,6 +384,13 @@
             return 0
 
         lax.fori_loop(1, RING, one, 0)
+
+    def later(f):
+        def one(i, _):
+            f(i)
+            return 0
+
+        lax.fori_loop(1, RING - y, one, 0)
 
     def states_out():
         arow[...] = dot_nt(decay_ref[...], tri(), lax.Precision.HIGHEST)
@@ -419,10 +428,10 @@
         state, decay = lax.fori_loop(0, RING, one, (jnp.zeros((64, ADH), F32), jnp.ones((1, ADH), F32)))
         tot_out[:64] = state.astype(BF)
         tot_out[64:] = split(decay)
-        every(lambda dy: column_copy(dy, False).start())
+        later(lambda dy: column_copy(dy, False).start())
 
     def incoming_out():
-        every(lambda dy: column_copy(dy, True).wait_recv())
+        lax.fori_loop(1, y + 1, lambda dy, _: (column_copy(dy, True).wait_recv(), 0)[1], 0)
 
         def one(i, state):
             block = tot_in[i]
@@ -640,7 +649,7 @@
                 if w_goes(dr, dist, pair):
                     w2(hf, dr, dist, pair, False).wait_send()
     every(lambda d: row_copy(st_out, st_in, st_s, st_r, d, False).wait_send())
-    every(lambda d: column_copy(d, False).wait_send())
+    later(lambda d: column_copy(d, False).wait_send())
     every(lambda d: row_copy(ret_out, ret_in, ret_s, ret_r, d, False).wait_send())
     for o in range(4):
         sib_copy(o).wait_send()
@@ -654,14 +663,13 @@
     x_in, gate_z, b_in, c_in, step_size, log_decay, d_skip, norm_gain, query, key, value, o_weight
 ):
     vmem = pl.BlockSpec(memory_space=pltpu.VMEM)
-    smem = pl.BlockSpec(memory_space=pltpu.SMEM)
     hbm = pl.BlockSpec(memory_space=pl.ANY)
     dma = pltpu.SemaphoreType.DMA
     tokens = (TOK, 512)
     return pl.pallas_call(
         kernel,
         out_shape=(jax.ShapeDtypeStruct(tokens, BF), jax.ShapeDtypeStruct(tokens, BF)),
-        in_specs=[hbm] * 6 + [smem, vmem] + [hbm] * 4,
+        in_specs=[hbm] * 7 + [vmem] + [hbm] * 4,
         out_specs=(vmem, vmem),
         scratch_shapes=[
             pltpu.VMEM(tokens, BF),
@@ -670,6 +678,7 @@
             pltpu.VMEM((TOK, ADH), BF),
             pltpu.VMEM((8, TOK), F32),
             pltpu.VMEM((8, TOK), F32),
+            pltpu.SMEM((8,), F32),
             pltpu.VMEM((2, RING, 2, TOK, ADH), BF),
             pltpu.VMEM((2, RING, 2, TOK, ADH), BF),
             pltpu.VMEM((2, RING, RING, 64, 256), BF),
@@ -701,7 +710,7 @@
             pltpu.VMEM((2, HALF, 512), BF),
             pltpu.VMEM((2,) + tokens, BF),
             pltpu.VMEM((2,) + tokens, BF),
-            dma((11,)), dma((8,)), dma((8,)), dma((2,)), dma((2,)), dma, dma, dma((2, 4, 2)), dma((2, 4, 2)),
+            dma((12,)), dma((8,)), dma((8,)), dma((2,)), dma((2,)), dma, dma, dma((2, 4, 2)), dma((2, 4, 2)),
             *[dma((2, 2, 4, 2))] * 6,
             dma((2, 8)), dma((2, 8)), dma((2, 2, 4, 4)), dma((2, 2, 4, 4)),
             dma((8,)), dma((8,)), dma((8,)), dma((8,)), dma((8,)), dma((8,)),

time: 101 us -> 101 us (level)
  no operation moved by 1% of the time
where the time goes in v4:
time: 101 us; the launch traced here: 100 us
  Pallas kernels  95.8 us (95%)
  local copies, waits for them, and re-layouts  3.67 us (4%)
    pallas_call x1, Pallas kernels, per_device(): pl.pallas_call(kernel, out_shape=(jax.ShapeDtypeStruct(tokens, BF), jax.S...  95.8 us
    unnamed x6, local copies, waits for them, and re-layouts  3.09 us

profile of v4, /device:TPU:1, one launch (start us, length us, event | category | flops | bytes accessed | tf_op | source)
XLA Modules:
  0.0 100.1 jit_solution(2390045250983887512)
XLA Ops:
  0.6 0.0 copy-start.1
  0.6 0.7 copy-done.1
  1.3 0.6 reshape.7.gain_ref
  1.9 95.8 %mixer_and_attention.1 = (bf16[256,512]{1,0:T(8,128)(2,1)}, bf16[256,512]{1,0:T(8,128)(2,1)}) custom-call(bf16[256,512]{1,0:T(8,128)(2,1)} %x_hbm.1, bf16[256,512]{1,0:T(8,128)(2,1)} %gate_hbm.1, bf16[256,128]{1,0:T(8,128)(2,1)} %b_hbm.1, bf16[256,128]{1,0:T(8,128)(2,1)} %c_hbm.1, f32[8,256]{1,0:T(8,128)} %step_hbm.1, f32[8,256]{1,0:T(8,128)} %decay_hbm.1, ...), custom_call_target="tpu_custom_call" | custom-call | tf_op jit(solution)/shard_map/mixer_and_attention/pallas_call | solution.py:669
  97.7 0.0 copy-start
  97.7 1.7 %copy.16 = bf16[256,512]{1,0:T(8,128)(2,1)} copy(bf16[256,512]{1,0:T(8,128)(2,1)} %get-tuple-element.4) | data formatting | bytes 524288
  99.4 0.0 copy-done
  99.4 0.7 copy.17
Async XLA Ops:
  0.6 0.7 copy-start.1
  97.7 1.7 %copy-start = (bf16[256,512]{1,0:T(8,128)(2,1)S(1)}, bf16[256,512]{1,0:T(8,128)(2,1)}, u32[]{:S(2)}) copy-start(bf16[256,512]{1,0:T(8,128)(2,1)} %get-tuple-element.5) | copy-start | bytes 786436
